TPU v7x, 256 devices: a whole 4x4x8 slice. The times are simulated.
256 devices in a mesh: seq: 64 (over z, y, core), head: 4 (over x).
Axes of the slice: x: 4, y: 4, z: 8, core: 2. Of those that a mesh axis runs over, the one named last changes fastest.
Arguments:
- queries: bfloat16 [16, 8192], P(None, 'head'), may hold values from -24 to 24
- keys: bfloat16 [16, 8192, 512], P(None, 'seq', 'head'), may hold values from -24 to 24
- values: bfloat16 [16, 8192, 512], P(None, 'seq', 'head'), may hold values from -8 to 8
- lengths: int32 [16], replicated, may hold values from 2 to 8192, as said below
- residual: bfloat16 [16, 4096], P(None, 'seq'), may hold values from -6 to 6
- out_weight: bfloat16 [8192, 4096], P('head', 'seq'), may hold values from -0.0625 to 0.0625
- norm_gain: float32 [4096], replicated, may hold values from 0.1 to 1.9
- expert_ids: int32 [16, 8], replicated, may hold values from 0 to 63, all different within a row; in each aligned block of 16 rows (0 to 15, 16 to 31, ...) at most 4 rows name the same one
- expert_gates: float32 [16, 8], replicated, may hold values from 0.05 to 0.5
- gate_weight: bfloat16 [64, 4096, 1536], P('seq', None, 'head'), may hold values from -0.09375 to 0.09375
- up_weight: bfloat16 [64, 4096, 1536], P('seq', None, 'head'), may hold values from -0.09375 to 0.09375
- down_weight: bfloat16 [64, 1536, 4096], P('seq', 'head'), may hold values from -0.4375 to 0.4375
Outputs:
- after_attention: bfloat16 [16, 4096], P(None, 'seq')
- layer_out: bfloat16 [16, 4096], P(None, ('seq', 'head'))
Inputs may be any that keep to these rules, and one draw needn't show every extreme that they name: `lengths`: at least one row has the full cache length 8192. `expert_ids`: each row names 8 different experts; every expert is named by some row; no expert is named by more than 4 rows, a bound that some block reaches.
All inputs are finite; a program needn't handle non-finite values.
Results may differ from a plain program's by a relative error of at most 0.012.
Values may be sent and summed in bfloat16 or wider, within the bound.
No kernel may reach another device: no remote copies, remote signals or barrier semaphores. Data moves between devices by JAX's collectives and lax.ppermute only.
A program may use at most 64 MiB of HBM per device.

v0:
```python
import math

import jax
import jax.numpy as jnp
from jax import lax
from jax.sharding import PartitionSpec as P

HD = 128


masked_value = -1e30


def joined(part, axis, combine):
    gathered = jax.tree.map(lambda a: lax.all_gather(a, axis), part)

    def take(source):
        return jax.tree.map(lambda a: lax.dynamic_index_in_dim(a, source, 0, False), gathered)

    return lax.fori_loop(
        1, lax.axis_size(axis), lambda source, state: combine(state, take(source)), take(0)
    )


def combine_parts(left_parts, right_parts):
    left_max, left_sum, left_numer = left_parts
    right_max, right_sum, right_numer = right_parts
    joined_max = jnp.maximum(left_max, right_max)
    left_scale = jnp.exp(left_max - joined_max)
    right_scale = jnp.exp(right_max - joined_max)
    joined_sum = left_sum * left_scale + right_sum * right_scale
    joined_numer = left_numer * left_scale[..., None] + right_numer * right_scale[..., None]
    return (joined_max, joined_sum, joined_numer)


def local(
    queries,
    keys,
    values,
    lengths,
    residual,
    out_weight,
    norm_gain,
    expert_ids,
    expert_gates,
    gate_weight,
    up_weight,
    down_weight,
):
    row_count = queries.shape[0]
    context_local = keys.shape[1]
    kv_local = keys.shape[2] // HD
    query_heads = queries.shape[1] // HD
    group_size = query_heads // kv_local
    query_grid = queries.reshape(row_count, kv_local, group_size, HD)
    key_grid = keys.reshape(row_count, context_local, kv_local, HD)
    value_grid = values.reshape(row_count, context_local, kv_local, HD)
    scores = jnp.einsum(
        "rkgd,rckd->rkgc", query_grid, key_grid, preferred_element_type=jnp.float32
    ) * (1.0 / math.sqrt(HD))
    positions = lax.axis_index("seq") * context_local + lax.iota(jnp.int32, context_local)
    valid_mask = (positions[None, :] < lengths[:, None])[:, None, None, :]
    block_max = jnp.max(jnp.where(valid_mask, scores, masked_value), axis=-1)
    weights = jnp.where(valid_mask, jnp.exp(scores - block_max[..., None]), 0.0).astype(
        jnp.bfloat16
    )
    block_sum = jnp.sum(weights.astype(jnp.float32), axis=-1)
    block_numer = jnp.einsum(
        "rkgc,rckd->rkgd", weights, value_grid, preferred_element_type=jnp.float32
    )
    joined_max, weight_total, numer_total = joined(
        (block_max, block_sum, block_numer), "seq", combine_parts
    )
    attention = (
        (numer_total / weight_total[..., None])
        .astype(jnp.bfloat16)
        .reshape(row_count, query_heads * HD)
    )
    partial_value = jnp.dot(attention, out_weight, preferred_element_type=jnp.float32)
    projected = lax.psum(partial_value, "head")
    after_local = (residual.astype(jnp.float32) + projected).astype(jnp.bfloat16)
    gathered = lax.all_gather(after_local, "seq", axis=1, tiled=True)
    after_wide = gathered.astype(jnp.float32)
    mean_square = jnp.mean(after_wide * after_wide, axis=-1, keepdims=True)
    normed = (after_wide * lax.rsqrt(mean_square + 1e-06) * norm_gain).astype(jnp.bfloat16)
    local_experts = gate_weight.shape[0]
    seq_count = lax.axis_size("seq")
    head_count = lax.axis_size("head")
    expert_index = lax.axis_index("seq") * local_experts + 0
    route_weight = jnp.sum(jnp.where(expert_ids == expert_index, expert_gates, 0.0), axis=1)
    gate_proj = jnp.dot(normed, gate_weight[0], preferred_element_type=jnp.float32)
    up_proj = jnp.dot(normed, up_weight[0], preferred_element_type=jnp.float32)
    hidden = (jax.nn.silu(gate_proj) * up_proj).astype(jnp.bfloat16)
    output = jnp.dot(hidden, down_weight[0], preferred_element_type=jnp.float32)
    weighted_outputs = (expert_index, route_weight[:, None] * output)
    piece_width = gathered.shape[1] // (seq_count * head_count)
    column_index = lax.axis_index("seq") * head_count + lax.axis_index("head")
    expert_index, weighted = weighted_outputs
    mixture = lax.psum_scatter(weighted, ("seq", "head"), scatter_dimension=1, tiled=True)
    own_after = lax.dynamic_slice_in_dim(gathered, column_index * piece_width, piece_width, 1)
    layer_out = (own_after.astype(jnp.float32) + mixture).astype(jnp.bfloat16)
    return (after_local, layer_out)


def solution(mesh):
    in_specs = (
        P(None, "head"),
        P(None, "seq", "head"),
        P(None, "seq", "head"),
        P(),
        P(None, "seq"),
        P("head", "seq"),
        P(),
        P(),
        P(),
        P("seq", None, "head"),
        P("seq", None, "head"),
        P("seq", "head", None),
    )
    out_specs = (P(None, "seq"), P(None, ("seq", "head")))
    return jax.shard_map(local, mesh=mesh, in_specs=in_specs, out_specs=out_specs, check_vma=False)
```

profile of v0, /device:TPU:1, one launch (start us, length us, event | category | flops | bytes accessed | tf_op | source)
XLA Modules:
  0.0 1567.7 jit_solution(5459959800023292364)
XLA Ops:
  9.0 1.5 select_reduce_fusion
  10.5 2.0 fusion.31
  12.6 54.9 %all-gather = f32[1024,16]{1,0:T(8,128)S(1)} all-gather(f32[16,16]{1,0:T(8,128)S(1)} %get-tuple-element.222), channel_id=2, replica_groups=mesh['seq'=64,'head'=4] {'seq'}, dimensions={0}, use_global_device_ids=true | all-gather | bytes 66560 | tf_op jit(solution)/shard_map/all_gather | solution.py:15
  68.5 49.2 %all-gather.1 = f32[1024,16]{1,0:T(8,128)S(1)} all-gather(f32[16,16]{1,0:T(8,128)S(1)} %convert_reduce_fusion), channel_id=3, replica_groups=mesh['seq'=64,'head'=4] {'seq'}, dimensions={0}, use_global_device_ids=true | all-gather | bytes 66560 | tf_op jit(solution)/shard_map/all_gather | solution.py:15
  118.6 1.2 select_reduce_fusion.1
  120.7 115.5 %while.19 = (s32[]{:T(128)}, f32[16,1,16]{2,1,0:T(1,128)S(1)}, f32[16,1,16]{2,1,0:T(1,128)S(1)}, f32[16,1,16,128]{3,2,1,0:T(8,128)S(1)}, f32[64,16,1,16]{3,1,2,0...) while((s32[]{:T(128)}, f32[16,1,16]{2,1,0:T(1,128)S(1)}, ...), condition=%wide.region_3.4_spmd, body=%wide.region_2.3_spmd.sunk | while | flops 99845 | bytes 407695 | solution.py:20
  121.5 1.1 fusion.39
  123.3 1.1 fusion.39
  125.1 1.1 fusion.39
  127.0 1.1 fusion.39
  128.8 1.1 fusion.39
  130.6 1.1 fusion.39
  132.5 1.1 fusion.39
  134.3 1.1 fusion.39
  136.1 1.1 fusion.39
  138.0 1.1 fusion.39
  139.8 1.1 fusion.39
  141.6 1.1 fusion.39
  143.5 1.1 fusion.39
  145.3 1.1 fusion.39
  147.1 1.1 fusion.39
  149.0 1.1 fusion.39
  150.8 1.1 fusion.39
  152.6 1.1 fusion.39
  154.5 1.1 fusion.39
  156.3 1.1 fusion.39
  158.1 1.1 fusion.39
  160.0 1.1 fusion.39
  161.8 1.1 fusion.39
  163.6 1.1 fusion.39
  165.5 1.1 fusion.39
  167.3 1.1 fusion.39
  169.1 1.1 fusion.39
  171.0 1.1 fusion.39
  172.8 1.1 fusion.39
  174.6 1.1 fusion.39
  176.5 1.1 fusion.39
  178.3 1.1 fusion.39
  180.1 1.1 fusion.39
  182.0 1.1 fusion.39
  183.8 1.1 fusion.39
  185.6 1.1 fusion.39
  187.5 1.1 fusion.39
  189.3 1.1 fusion.39
  193.0 1.1 fusion.39
  194.8 1.1 fusion.39
  196.7 1.1 fusion.39
  202.2 1.1 fusion.39
  204.0 1.1 fusion.39
  205.8 1.1 fusion.39
  211.3 1.1 fusion.39
  213.2 1.1 fusion.39
  215.0 1.1 fusion.39
  224.2 1.1 fusion.39
  226.0 1.1 fusion.39
  231.5 1.1 fusion.39
  233.3 1.1 fusion.39
  235.2 1.1 fusion.39
  236.6 8.7 psum.7
  245.9 43.8 %all-gather.3 = bf16[64,64,16]{1,2,0:T(8,128)(2,1)S(1)} all-gather(bf16[1,64,16]{1,2,0:T(8,128)(2,1)S(1)} %bitcast.116), channel_id=1, replica_groups=mesh['seq'=64,'head'=4] {'seq'}, dimensions={0}, use_global_device_ids=true | all-gather | bytes 133120 | tf_op jit(solution)/shard_map/all_gather | solution.py:82
  290.8 3.1 fusion.4
  293.9 3.2 convolution_multiply_fusion
  297.1 2.0 copy.22
  299.1 1260.3 %reduce-scatter.4.cloned.1.call-done = f32[16,16]{1,0:T(8,128)} async-done(((f32[4096,16]{1,0:T(8,128)}), f32[16,16]{1,0:T(8,128)}) %reduce-scatter.4.cloned.1.call-update) | async-done | bytes 1040
  (174 shorter events, 66.1 us)
Async XLA Ops:
  7.2 286.7 %copy-start = (bf16[1,384,4096]{2,1,0:T(8,128)(2,1)S(1)}, bf16[1,384,4096]{2,1,0:T(8,128)(2,1)}, u32[]{:S(2)}) copy-start(bf16[1,384,4096]{2,1,0:T(8,128)(2,1)} %param.25) | copy-start | bytes 9437188
  7.2 112.6 %all-gather.6.cloned.1.call-start = ((), (), s32[]{:S(2)}) async-start(), calls=%async_computation.1 | async-start | bytes 8519680 | tf_op jit(solution)/shard_map/all_gather | solution.py:15
  9.0 3.6 copy-start.5
  9.0 227.4 %copy-start.3 = (bf16[2048,64]{0,1:T(8,128)(2,1)S(1)}, bf16[2048,64]{0,1:T(8,128)(2,1)}, u32[]{:S(2)}) copy-start(bf16[2048,64]{0,1:T(8,128)(2,1)} %param.19) | copy-start | bytes 786436
  12.6 1546.9 %reduce-scatter.4.cloned.1.call-start = ((), (), s32[]{:S(2)}) async-start(), calls=%async_computation.2 | async-start | bytes 2105344
  67.6 0.9 copy-start.1
  117.7 0.9 copy-start.2
  236.6 57.3 %copy-start.4 = (f32[4096]{0:T(1024)S(1)}, f32[4096]{0:T(1024)}, u32[]{:S(2)}) copy-start(f32[4096]{0:T(1024)} %param.20) | copy-start | bytes 49156
  245.9 43.8 %copy-start.6 = (bf16[16,64]{1,0:T(8,128)(2,1)}, bf16[16,64]{1,0:T(8,128)(2,1)S(1)}, u32[]{:S(2)}) copy-start(bf16[16,64]{1,0:T(8,128)(2,1)S(1)} %add_convert_fusion) | copy-start | bytes 6148
  290.2 0.6 copy-start.7
Sparse Core Ops, SparseCore 0:
  12.7 87.4 all-gather.5
  299.3 1260.1 reduce-scatter.3
where the time goes:
time: 1580 us; the launch traced here: 1570 us
  waiting for transfers between devices  1260 us (80%)
  blocking collectives  157 us (10%)
  other arithmetic  72.9 us (5%)
  local copies, waits for them, and re-layouts  51.9 us (3%)
    unnamed x3, waiting for transfers between devices  1260 us
    all_gather x2, blocking collectives, joined(): gathered = jax.tree.map(lambda a: lax.all_gather(a, axis), part)  104 us
    add x63, other arithmetic, combine_parts(): left_numer * left_scale[..., None] + right_numer * right_scale[..., None]  67.6 us
    dynamic_slice x65, local copies, waits for them, and re-layouts, take(): lax.dynamic_index_in_dim(a, source, 0, False)  45.5 us
    all_gather x1, blocking collectives, local(): gathered = lax.all_gather(after_local, 'seq', axis=1, tiled=True)  43.8 us
  transfers between devices with their start and end apart: 2, of which 1 were waited for; matrix products, arithmetic and copies ran while one was open for 0% of the time, Pallas kernels for 0%

commit v1 on v0

v1 whole, which is shorter than its diff:
```python
import math

import jax
import jax.numpy as jnp
from jax import lax
from jax.experimental import pallas as pl
from jax.experimental.pallas import tpu as pltpu
from jax.sharding import PartitionSpec as P

HD = 128
LANES = 128
SLOTS = 4
MASKED = -1e30
CHUNKS = 4
F32 = jnp.float32
BF16 = jnp.bfloat16
NT = (((1,), (1,)), ((), ()))
TN = (((0,), (0,)), ((), ()))


def iota(shape, dim):
    return lax.broadcasted_iota(jnp.int32, shape, dim)


def call(body, outs, args, hbm=(), results=(), scratch=(), limit=8 << 20):
    spaces = [pltpu.HBM if i in hbm else pltpu.VMEM for i in range(len(args))]
    args = [pltpu.with_memory_space_constraint(a, s) for a, s in zip(args, spaces)]
    return pl.pallas_call(
        body,
        out_shape=[
            jax.ShapeDtypeStruct(shape, dtype) if i in results else pltpu.VMEM(shape, dtype)
            for i, (shape, dtype) in enumerate(outs)
        ],
        in_specs=[pl.BlockSpec(memory_space=s) for s in spaces],
        out_specs=[pl.BlockSpec(memory_space=pltpu.VMEM) for _ in outs],
        scratch_shapes=list(scratch),
        compiler_params=pltpu.CompilerParams(vmem_limit_bytes=limit),
    )(*args)


def attend(lengths_hbm, q_hbm, k_hbm, v_hbm, *refs):
    lengths, q, k, v, wide, cache_sems, later_sems = refs[-7:]
    later = (len(refs) - 8) // 2
    out = refs[later]
    rows, heads = q.shape[0], q.shape[1] // HD
    chunk = rows // CHUNKS
    fetch_q = pltpu.make_async_copy(q_hbm, q, cache_sems.at[2 * CHUNKS])
    fetch_q.start()
    fetch_lengths = pltpu.make_async_copy(lengths_hbm, lengths, cache_sems.at[2 * CHUNKS + 1])
    fetch_lengths.start()
    fetch_k, fetch_v = [], []
    for c in range(CHUNKS):
        part = pl.ds(c * chunk, chunk)
        fetch_k.append(pltpu.make_async_copy(k_hbm.at[part], k.at[part], cache_sems.at[c]))
        fetch_k[c].start()
        fetch_v.append(pltpu.make_async_copy(v_hbm.at[part], v.at[part], cache_sems.at[CHUNKS + c]))
        fetch_v[c].start()
    fetch_later = []
    for i in range(later):
        fetch_later.append(pltpu.make_async_copy(refs[i], refs[later + 1 + i], later_sems.at[i]))
        fetch_later[i].start()
    fetch_q.wait()
    for h in range(heads):
        x = q[:, h * HD : (h + 1) * HD].astype(F32)
        at = (h // SLOTS) * 2 * SLOTS + h % SLOTS
        wide[pl.ds(at * rows, rows), :] = x
        wide[pl.ds((at + SLOTS) * rows, rows), :] = x
    fetch_lengths.wait()
    first = lax.axis_index("seq") * k.shape[1]
    tall = 2 * heads
    place = first + iota((tall, k.shape[1]), 1)
    lane = iota((chunk * tall, LANES), 1)
    upper = iota((chunk * tall, LANES), 0) % (2 * SLOTS) < SLOTS
    for c in range(CHUNKS):
        members = range(c * chunk, (c + 1) * chunk)
        fetch_k[c].wait()
        scores = [
            lax.dot_general(
                wide[pl.ds(r, tall, stride=rows), :].astype(BF16), k[r], NT, preferred_element_type=F32
            )
            for r in members
        ]
        scores = jnp.concatenate(scores, axis=0) * (1.0 / math.sqrt(HD))
        valid = jnp.concatenate([place < lengths[r] for r in members], axis=0)
        top = jnp.max(jnp.where(valid, scores, MASKED), axis=1, keepdims=True).astype(BF16).astype(F32)
        weights = jnp.where(valid, jnp.exp(scores - top), 0.0).astype(BF16)
        total = jnp.sum(weights.astype(F32), axis=1, keepdims=True)
        fetch_v[c].wait()
        numer = [
            jnp.dot(weights[i * tall : (i + 1) * tall], v[r], preferred_element_type=F32)
            for i, r in enumerate(members)
        ]
        high = total.astype(BF16).astype(F32)
        stats = jnp.where(lane < 64, top, jnp.where(lane < 96, high, total - high))
        block = jnp.where(upper, jnp.concatenate(numer, axis=0), stats)
        out[pl.ds(c * chunk * tall, chunk * tall), :] = block.astype(BF16)
    for copy in fetch_later:
        copy.wait()


def combine(parts, out):
    count = parts.shape[0] // (2 * SLOTS)
    x = parts[...].astype(F32).reshape(count, 2 * SLOTS, LANES)
    numer, stats = x[:, :SLOTS], x[:, SLOTS:]
    top = stats[:, :, 0:1]
    total = stats[:, :, 64:65] + stats[:, :, 96:97]
    scale = jnp.exp(top - jnp.max(top, axis=0, keepdims=True))
    joined = jnp.sum(scale * numer, axis=0) / jnp.sum(scale * total, axis=0)
    pair = jnp.concatenate([joined, joined], axis=0)
    out[...] = jnp.broadcast_to(pair[None], (count // 2, 2 * SLOTS, LANES)).reshape(out.shape).astype(BF16)


def project(pieces, weight, out, wide):
    rows = 2 * out.shape[1]
    heads = pieces.shape[0] // rows
    wide[...] = pieces[...].astype(F32)
    lhs = jnp.concatenate(
        [wide[pl.ds(h, rows, stride=heads), :].astype(BF16) for h in range(heads)], axis=1
    )
    part = lax.dot_general(lhs, weight[...], NT, preferred_element_type=F32)
    halves = jnp.concatenate([part[: rows // 2], part[rows // 2 :]], axis=1)
    out[...] = jnp.broadcast_to(halves[None], out.shape)


def selection(ids, count, copies):
    top_k, rows = ids.shape
    shape = (count * copies * 2, 2 * rows)
    expert = iota(shape, 0) // (2 * copies)
    wide = jnp.concatenate([ids, ids], axis=1)
    hit = expert == wide[0:1, :]
    for k in range(1, top_k):
        hit = hit | (expert == wide[k : k + 1, :])
    hit = hit.astype(F32)
    square = (2 * rows, 2 * rows)
    before = (iota(square, 0) < iota(square, 1) % rows).astype(F32)
    rank = jnp.dot(hit, before, preferred_element_type=F32)
    slot = iota(shape, 0) % 2 + 2 * (iota(shape, 1) // rows)
    return jnp.where(rank == slot.astype(F32), hit, 0.0).astype(BF16)


def residual_step(parts, residual, ids, after, out):
    total = parts[0]
    for i in range(1, parts.shape[0]):
        total = total + parts[i]
    total = jnp.concatenate([total[:, : LANES // 2], total[:, LANES // 2 :]], axis=0)
    own = (residual[...].astype(F32) + total).astype(BF16)
    after[...] = own
    own = own.astype(F32)
    none = jnp.zeros_like(own)
    twice = jnp.concatenate(
        [jnp.concatenate([own, none], axis=1), jnp.concatenate([none, own], axis=1)], axis=0
    ).astype(BF16)
    pick = selection(ids[...], out.shape[0] // 2, 1)
    out[...] = jnp.dot(pick, twice, preferred_element_type=F32).astype(BF16)


def swap(y):
    count = y.shape[0]
    row = iota(y.shape, 0) % 4
    lane = iota(y.shape, 1)
    z = pltpu.roll(y, 64, 1)
    up = pltpu.roll(z, count - 2, 0)
    down = pltpu.roll(z, 2, 0)
    return jnp.where(lane < 64, jnp.where(row < 2, y, down), jnp.where(row < 2, up, y))


def experts(pieces, gain, gate, up, down, ids, gates, out):
    width = gain.shape[1]
    blocks = width // LANES
    stacked = swap(pieces[...].astype(F32))
    tiles = []
    for b in range(blocks):
        tile = stacked[8 * (b // 2) : 8 * (b // 2) + 8]
        tiles.append(tile if b % 2 == 0 else pltpu.roll(tile, 4, 0))
    x = jnp.concatenate(tiles, axis=1)
    square = jnp.sum(x * x, axis=1, keepdims=True) * (1.0 / width)
    normed = (x * lax.rsqrt(square + 1e-6) * gain[...]).astype(BF16)
    gate_proj = jnp.dot(normed, gate[0], preferred_element_type=F32)
    up_proj = jnp.dot(normed, up[0], preferred_element_type=F32)
    hidden = (gate_proj / (1.0 + jnp.exp(-gate_proj)) * up_proj).astype(BF16)
    result = jnp.dot(hidden, down[0], preferred_element_type=F32)

    rows = ids.shape[1]
    mine = ids[...] == lax.axis_index("seq")
    route = jnp.sum(jnp.where(mine, gates[...], 0.0), axis=0, keepdims=True)
    named = jnp.max(mine.astype(F32), axis=0, keepdims=True)
    named = jnp.broadcast_to(named, (8, rows))
    before = (iota((rows, rows), 0) < iota((rows, rows), 1)).astype(F32)
    rank = jnp.dot(named, before, preferred_element_type=F32)
    chosen = (rank == iota((8, rows), 0).astype(F32)) & (named > 0.0)
    result = result * jnp.sum(jnp.where(chosen, route, 0.0), axis=1, keepdims=True)

    lower = iota((8, LANES), 0) < 4
    pairs = []
    for b in range(0, blocks, 2):
        left = result[:, b * LANES : (b + 1) * LANES]
        right = result[:, (b + 1) * LANES : (b + 2) * LANES]
        pairs.append(jnp.where(lower, left, pltpu.roll(right, 4, 0)))
    packed = swap(jnp.concatenate(pairs, axis=0)).astype(BF16)
    shape = (out.shape[0], packed.shape[0])
    copies = out.shape[0] // packed.shape[0]
    target, source = iota(shape, 0), iota(shape, 1)
    repeat = (target // (2 * copies) == source // 2) & (target % 2 == source % 2)
    out[...] = jnp.dot(repeat.astype(BF16), packed, preferred_element_type=F32).astype(BF16)


def finish(pieces, after, ids, out):
    rows, width = out.shape
    pick = selection(ids[...], 64, pieces.shape[0] // 128)
    mixed = lax.dot_general(pick, pieces[...], TN, preferred_element_type=F32)
    mixture = mixed[:rows] + pltpu.roll(mixed[rows:], 64, 1)
    own = after[...].astype(F32)
    total = mixture + jnp.concatenate([own, jnp.zeros_like(own)], axis=1)
    shift = (LANES - width * lax.axis_index("head")) % LANES
    out[...] = pltpu.roll(total, shift, 1)[:, :width].astype(BF16)


def exchange(x, axis):
    return lax.all_to_all(x, axis, 0, 0, tiled=True)


def local(
    queries,
    keys,
    values,
    lengths,
    residual,
    out_weight,
    norm_gain,
    expert_ids,
    expert_gates,
    gate_weight,
    up_weight,
    down_weight,
):
    seq, head = lax.axis_size("seq"), lax.axis_size("head")
    rows = queries.shape[0]
    ids, gates = expert_ids.T, expert_gates.T

    later = [out_weight.T, residual, norm_gain.reshape(1, -1), ids, gates, gate_weight, up_weight, down_weight]
    parts, *later = call(
        attend,
        [((seq * 2 * SLOTS, LANES), BF16)] + [(a.shape, a.dtype) for a in later],
        [lengths, queries, keys, values, *later],
        hbm=range(4 + len(later)),
        scratch=[
            pltpu.SMEM(lengths.shape, lengths.dtype),
            pltpu.VMEM(queries.shape, BF16),
            pltpu.VMEM(keys.shape, BF16),
            pltpu.VMEM(values.shape, BF16),
            pltpu.VMEM((2 * queries.shape[1] // HD * rows, HD), F32),
            pltpu.SemaphoreType.DMA((2 * CHUNKS + 2,)),
            pltpu.SemaphoreType.DMA((len(later),)),
        ],
    )
    weight, residual, gain, ids, gates, gate_weight, up_weight, down_weight = later
    parts = exchange(parts, "seq")
    (joined,) = call(combine, [((seq * SLOTS, LANES), BF16)], [parts])
    joined = exchange(joined, "seq")
    (projected,) = call(
        project,
        [((head, rows // 2, LANES), F32)],
        [joined, weight],
        scratch=[pltpu.VMEM((seq * SLOTS, LANES), F32)],
    )
    summands = exchange(projected, "head")
    after, chosen = call(
        residual_step,
        [(residual.shape, BF16), ((seq * 2, LANES), BF16)],
        [summands, residual, ids],
    )
    chosen = exchange(chosen, "seq")
    (outputs,) = call(
        experts,
        [((seq * head * 2, LANES), BF16)],
        [chosen, gain, gate_weight, up_weight, down_weight, ids, gates],
    )
    outputs = exchange(outputs, ("seq", "head"))
    (layer_out,) = call(
        finish, [((rows, residual.shape[1] // head), BF16)], [outputs, after, ids], results=(0,)
    )
    return after, layer_out


def solution(mesh):
    in_specs = (
        P(None, "head"),
        P(None, "seq", "head"),
        P(None, "seq", "head"),
        P(),
        P(None, "seq"),
        P("head", "seq"),
        P(),
        P(),
        P(),
        P("seq", None, "head"),
        P("seq", None, "head"),
        P("seq", "head", None),
    )
    out_specs = (P(None, "seq"), P(None, ("seq", "head")))
    return jax.shard_map(local, mesh=mesh, in_specs=in_specs, out_specs=out_specs, check_vma=False)
```

time: 1580 us -> 89.3 us (0.06)
  waiting for transfers between devices: 1260 us -> 12.3 us
  blocking collectives: 157 us -> 60.5 us
  other arithmetic: 72.9 us -> 0 us
  local copies, waits for them, and re-layouts: 51.9 us -> 0.6 us
    unnamed x3 -> x0, waiting for transfers between devices: 1260 us -> none
    all_gather x3 -> x0, blocking collectives: 148 us -> none  [the longest x2 104 us: joined(): gathered = jax.tree.map(lambda a: lax.all_gather(a, axis), part)]
    add x127 -> x0, other arithmetic: 68.4 us -> none  [the longest x63 67.6 us: combine_parts(): left_numer * left_scale[..., None] + right_numer * right_scale[..., None]]
    all_to_all x0 -> x4, blocking collectives: none -> 60.5 us  [exchange(): return lax.all_to_all(x, axis, 0, 0, tiled=True)]
    dynamic_slice x65 -> x0, local copies, waits for them, and re-layouts: 45.5 us -> none  [take(): lax.dynamic_index_in_dim(a, source, 0, False)]
  transfers between devices with their start and end apart: 2 -> 1, of which waited for: 1 -> 1; matrix products, arithmetic and copies ran while one was open for 0% -> 1% of each run, Pallas kernels for 0% -> 0%
where the time goes in v1:
time: 89.3 us; the launch traced here: 89 us
  blocking collectives  60.5 us (68%)
  waiting for transfers between devices  12.3 us (14%)
  Pallas kernels  9.28 us (10%)
  starting transfers between devices  5.66 us (6%)
    all_to_all x4, blocking collectives, exchange(): return lax.all_to_all(x, axis, 0, 0, tiled=True)  60.5 us
    all_to_all x1, waiting for transfers between devices, exchange(): return lax.all_to_all(x, axis, 0, 0, tiled=True)  12.3 us
    pallas_call x6, Pallas kernels, call(): pl.pallas_call(body, out_shape=[jax.ShapeDtypeStruct(shape, dtype) if i i...  9.28 us
    all_to_all x1, starting transfers between devices, exchange(): return lax.all_to_all(x, axis, 0, 0, tiled=True)  5.66 us
  transfers between devices with their start and end apart: 1, of which 1 were waited for; matrix products, arithmetic and copies ran while one was open for 1% of the time, Pallas kernels for 0%

profile of v1, /device:TPU:1, one launch (start us, length us, event | category | flops | bytes accessed | tf_op | source)
XLA Modules:
  0.0 89.0 jit_solution(8938112202198506785)
XLA Ops:
  0.6 4.4 %shard_map.131 = (bf16[512,128]{1,0:T(8,128)(2,1)S(1)}, bf16[64,2048]{1,0:T(8,128)(2,1)S(1)}, bf16[16,64]{1,0:T(8,128)(2,1)S(1)}, f32[1,4096]{1,0:T(1,128)S(1)},...) custom-call(s32[16]{0:T(128)} %lengths_hbm.1, ...), custom_call_target="tpu_custom_call" | custom-call | tf_op jit(solution)/shard_map/pallas_call | solution.py:28
  5.1 24.1 %all_to_all.49 = bf16[64,8,128]{2,1,0:T(8,128)(2,1)S(1)} all-to-all(bf16[64,8,128]{2,1,0:T(8,128)(2,1)S(1)} %bitcast.17), channel_id=1, replica_groups=mesh['seq'=64,'head'=4] {'seq'}, dimensions={0} | all-to-all | bytes 262144 | tf_op jit(solution)/shard_map/all_to_all | solution.py:219
  29.2 0.3 shard_map.132
  29.4 13.9 %all_to_all.50 = bf16[64,4,128]{2,1,0:T(4,128)(2,1)S(1)} all-to-all(bf16[64,4,128]{2,1,0:T(4,128)(2,1)S(1)} %bitcast.14), channel_id=1, replica_groups=mesh['seq'=64,'head'=4] {'seq'}, dimensions={0} | all-to-all | bytes 131072 | tf_op jit(solution)/shard_map/all_to_all | solution.py:219
  43.3 0.3 shard_map.133
  43.6 8.0 %all_to_all.51.parts = f32[4,8,128]{2,1,0:T(8,128)S(1)} all-to-all(f32[4,8,128]{2,1,0:T(8,128)S(1)} %shard_map.133), channel_id=1, replica_groups=mesh['seq'=64,'head'=4] {'head'}, dimensions={0} | all-to-all | bytes 32768 | tf_op jit(solution)/shard_map/all_to_all | solution.py:219
  51.6 0.4 shard_map.134
  52.0 14.5 %all_to_all.52 = bf16[64,2,128]{2,1,0:T(2,128)(2,1)S(1)} all-to-all(bf16[64,2,128]{2,1,0:T(2,128)(2,1)S(1)} %bitcast.18), channel_id=1, replica_groups=mesh['seq'=64,'head'=4] {'seq'}, dimensions={0} | all-to-all | bytes 65536 | tf_op jit(solution)/shard_map/all_to_all | solution.py:219
  66.5 2.6 %shard_map.135 = bf16[512,128]{1,0:T(8,128)(2,1)} custom-call(bf16[128,128]{1,0:T(8,128)(2,1)S(1)} %bitcast.16, f32[1,4096]{1,0:T(1,128)S(1)} %get-tuple-element.19.gain, bf16[1,4096,384]{2,1,0:T(8,128)(2,1)S(1)} %get-tuple-element.20.gate, bf16[1,4096,384]{2,1,0:T(8,128)(2,1)S(1)} %get-tuple-element.21.up, ...), custom_call_target="tpu_custom_call" | custom-call | tf_op jit(solution)/shard_map/pallas_call | solution.py:28
  69.1 5.7 %all-to-all-start.4 = ((bf16[256,2,128]{2,1,0:T(2,128)(2,1)}), bf16[256,2,128]{2,1,0:T(2,128)(2,1)S(1)}, u32[]{:S(2)}, u32[]{:S(2)}) async-start(bf16[256,2,128]{2,1,0:T(2,128)(2,1)} %bitcast.10), calls=%async_computation.4 | async-start | bytes 262144 | tf_op jit(solution)/shard_map/all_to_all | solution.py:219
  74.8 0.6 copy.14
  75.4 12.3 %all-to-all-done.4 = bf16[256,2,128]{2,1,0:T(2,128)(2,1)S(1)} async-done(((bf16[256,2,128]{2,1,0:T(2,128)(2,1)}), bf16[256,2,128]{2,1,0:T(2,128)(2,1)S(1)}, u32[]{:S(2)}, u32[]{:S(2)}) %all-to-all-start.4) | async-done | bytes 131104 | tf_op jit(solution)/shard_map/all_to_all | solution.py:219
  87.7 1.3 %shard_map.136 = bf16[16,16]{1,0:T(8,128)(2,1)} custom-call(bf16[512,128]{1,0:T(8,128)(2,1)S(1)} %bitcast.12, bf16[16,64]{1,0:T(8,128)(2,1)S(1)} %get-tuple-element.24.after, s32[8,16]{1,0:T(8,128)S(1)} %get-tuple-element.16.ids), custom_call_target="tpu_custom_call" | custom-call | tf_op jit(solution)/shard_map/pallas_call | solution.py:28
Async XLA Ops:
  69.1 18.6 %all-to-all-start.4 = ((bf16[256,2,128]{2,1,0:T(2,128)(2,1)}), bf16[256,2,128]{2,1,0:T(2,128)(2,1)S(1)}, u32[]{:S(2)}, u32[]{:S(2)}) async-start(bf16[256,2,128]{2,1,0:T(2,128)(2,1)} %bitcast.10), calls=%async_computation.4 | async-start | bytes 262144 | tf_op jit(solution)/shard_map/all_to_all | solution.py:219

commit v2 on v1

--- a/solution.py
+++ b/solution.py
@@ -11,7 +11,8 @@
 LANES = 128
 SLOTS = 4
 MASKED = -1e30
-CHUNKS = 4
+CHUNKS = 1
+STREAMS = 4
 F32 = jnp.float32
 BF16 = jnp.bfloat16
 NT = (((1,), (1,)), ((), ()))
@@ -22,7 +23,7 @@
     return lax.broadcasted_iota(jnp.int32, shape, dim)
 
 
-def call(body, outs, args, hbm=(), results=(), scratch=(), limit=8 << 20):
+def call(body, outs, args, hbm=(), results=(), scratch=(), limit=16 << 20):
     spaces = [pltpu.HBM if i in hbm else pltpu.VMEM for i in range(len(args))]
     args = [pltpu.with_memory_space_constraint(a, s) for a, s in zip(args, spaces)]
     return pl.pallas_call(
@@ -110,22 +111,29 @@
     out[...] = jnp.broadcast_to(pair[None], (count // 2, 2 * SLOTS, LANES)).reshape(out.shape).astype(BF16)
 
 
-def project(pieces, weight, out, wide):
-    rows = 2 * out.shape[1]
+def project(pieces, weight, residual, ids, out, pick, wide):
+    rows = residual.shape[0]
     heads = pieces.shape[0] // rows
     wide[...] = pieces[...].astype(F32)
     lhs = jnp.concatenate(
         [wide[pl.ds(h, rows, stride=heads), :].astype(BF16) for h in range(heads)], axis=1
     )
     part = lax.dot_general(lhs, weight[...], NT, preferred_element_type=F32)
-    halves = jnp.concatenate([part[: rows // 2], part[rows // 2 :]], axis=1)
-    out[...] = jnp.broadcast_to(halves[None], out.shape)
-
-
-def selection(ids, count, copies):
+    part = part + jnp.where(lax.axis_index("head") == 0, residual[...].astype(F32), 0.0)
+    none = jnp.zeros_like(part)
+    twice = jnp.concatenate(
+        [jnp.concatenate([part, none], axis=1), jnp.concatenate([none, part], axis=1)], axis=0
+    ).astype(BF16)
+    chosen = selection(ids[...], pick.shape[0] // 2)
+    pick[...] = chosen
+    send = jnp.dot(chosen, twice, preferred_element_type=F32).astype(BF16)
+    out[...] = jnp.concatenate([send] * (out.shape[0] // send.shape[0]), axis=0)
+
+
+def selection(ids, count):
     top_k, rows = ids.shape
-    shape = (count * copies * 2, 2 * rows)
-    expert = iota(shape, 0) // (2 * copies)
+    shape = (count * 2, 2 * rows)
+    expert = iota(shape, 0) // 2
     wide = jnp.concatenate([ids, ids], axis=1)
     hit = expert == wide[0:1, :]
     for k in range(1, top_k):
@@ -138,22 +146,6 @@
     return jnp.where(rank == slot.astype(F32), hit, 0.0).astype(BF16)
 
 
-def residual_step(parts, residual, ids, after, out):
-    total = parts[0]
-    for i in range(1, parts.shape[0]):
-        total = total + parts[i]
-    total = jnp.concatenate([total[:, : LANES // 2], total[:, LANES // 2 :]], axis=0)
-    own = (residual[...].astype(F32) + total).astype(BF16)
-    after[...] = own
-    own = own.astype(F32)
-    none = jnp.zeros_like(own)
-    twice = jnp.concatenate(
-        [jnp.concatenate([own, none], axis=1), jnp.concatenate([none, own], axis=1)], axis=0
-    ).astype(BF16)
-    pick = selection(ids[...], out.shape[0] // 2, 1)
-    out[...] = jnp.dot(pick, twice, preferred_element_type=F32).astype(BF16)
-
-
 def swap(y):
     count = y.shape[0]
     row = iota(y.shape, 0) % 4
@@ -164,10 +156,23 @@
     return jnp.where(lane < 64, jnp.where(row < 2, y, down), jnp.where(row < 2, up, y))
 
 
-def experts(pieces, gain, gate, up, down, ids, gates, out):
+def experts(pieces, gain, down, ids, gates, gate_hbm, up_hbm, out, gate, up, sems):
     width = gain.shape[1]
     blocks = width // LANES
-    stacked = swap(pieces[...].astype(F32))
+    depth = gate.shape[0] // STREAMS
+    fetch = []
+    for i in range(STREAMS):
+        part = pl.ds(i * depth, depth)
+        fetch.append(pltpu.make_async_copy(gate_hbm.at[0, part], gate.at[part], sems.at[2 * i]))
+        fetch.append(pltpu.make_async_copy(up_hbm.at[0, part], up.at[part], sems.at[2 * i + 1]))
+    for copy in fetch:
+        copy.start()
+    half = 2 * lax.axis_size("seq")
+    heads = pieces.shape[0] // half
+    summed = pieces[:half].astype(F32)
+    for i in range(1, heads):
+        summed = summed + pieces[i * half : (i + 1) * half].astype(F32)
+    stacked = swap(summed).astype(BF16).astype(F32)
     tiles = []
     for b in range(blocks):
         tile = stacked[8 * (b // 2) : 8 * (b // 2) + 8]
@@ -175,8 +180,13 @@
     x = jnp.concatenate(tiles, axis=1)
     square = jnp.sum(x * x, axis=1, keepdims=True) * (1.0 / width)
     normed = (x * lax.rsqrt(square + 1e-6) * gain[...]).astype(BF16)
-    gate_proj = jnp.dot(normed, gate[0], preferred_element_type=F32)
-    up_proj = jnp.dot(normed, up[0], preferred_element_type=F32)
+    gate_proj = up_proj = jnp.zeros((normed.shape[0], gate.shape[1]), F32)
+    for i in range(STREAMS):
+        part = slice(i * depth, (i + 1) * depth)
+        fetch[2 * i].wait()
+        gate_proj = gate_proj + jnp.dot(normed[:, part], gate[part], preferred_element_type=F32)
+        fetch[2 * i + 1].wait()
+        up_proj = up_proj + jnp.dot(normed[:, part], up[part], preferred_element_type=F32)
     hidden = (gate_proj / (1.0 + jnp.exp(-gate_proj)) * up_proj).astype(BF16)
     result = jnp.dot(hidden, down[0], preferred_element_type=F32)
 
@@ -196,23 +206,36 @@
         left = result[:, b * LANES : (b + 1) * LANES]
         right = result[:, (b + 1) * LANES : (b + 2) * LANES]
         pairs.append(jnp.where(lower, left, pltpu.roll(right, 4, 0)))
-    packed = swap(jnp.concatenate(pairs, axis=0)).astype(BF16)
-    shape = (out.shape[0], packed.shape[0])
-    copies = out.shape[0] // packed.shape[0]
-    target, source = iota(shape, 0), iota(shape, 1)
-    repeat = (target // (2 * copies) == source // 2) & (target % 2 == source % 2)
-    out[...] = jnp.dot(repeat.astype(BF16), packed, preferred_element_type=F32).astype(BF16)
-
-
-def finish(pieces, after, ids, out):
+    mixed = jnp.concatenate(pairs, axis=0)
+    head = lax.axis_index("head")
+    group = iota(mixed.shape, 1) // 16 % heads
+    moved = pltpu.roll(stacked, jnp.where(head % 2 == 0, 16, LANES - 16), 1)
+    for target in range(heads):
+        carried = jnp.where(target == head, moved, stacked)
+        packed = swap(jnp.where(group == target, mixed, carried))
+        out[pl.ds(target * half, half), :] = packed.astype(BF16)
+
+
+def finish(pieces, pick, ids, after, out):
+    half = pick.shape[0]
     rows, width = out.shape
-    pick = selection(ids[...], 64, pieces.shape[0] // 128)
-    mixed = lax.dot_general(pick, pieces[...], TN, preferred_element_type=F32)
-    mixture = mixed[:rows] + pltpu.roll(mixed[rows:], 64, 1)
-    own = after[...].astype(F32)
-    total = mixture + jnp.concatenate([own, jnp.zeros_like(own)], axis=1)
-    shift = (LANES - width * lax.axis_index("head")) % LANES
-    out[...] = pltpu.roll(total, shift, 1)[:, :width].astype(BF16)
+    heads = pieces.shape[0] // half
+    chosen = pick[...]
+    first = jnp.concatenate([ids[0:1, :], ids[0:1, :]], axis=1) == iota(chosen.shape, 0) // 2
+    both = jnp.concatenate([chosen.astype(F32), jnp.where(first, chosen.astype(F32), 0.0)], axis=1).astype(BF16)
+    head = lax.axis_index("head")
+    group = iota((rows, LANES), 1) // 16
+    mixture = jnp.zeros((rows, LANES), F32)
+    own = jnp.zeros((rows, LANES), F32)
+    for source in range(heads):
+        got = lax.dot_general(both, pieces[source * half : (source + 1) * half], TN, preferred_element_type=F32)
+        mixture = mixture + got[:rows] + pltpu.roll(got[rows : 2 * rows], 64, 1)
+        carried = got[2 * rows : 3 * rows] + pltpu.roll(got[3 * rows :], 64, 1)
+        moved = pltpu.roll(carried, LANES - 16 if source % 2 == 0 else 16, 1)
+        own = own + jnp.where(group == source, jnp.where(head == source, moved, carried), 0.0)
+    after[...] = own[:, : after.shape[1]].astype(BF16)
+    shift = (LANES - width * head) % LANES
+    out[...] = pltpu.roll(mixture + own, shift, 1)[:, :width].astype(BF16)
 
 
 def exchange(x, axis):
@@ -237,7 +260,7 @@
     rows = queries.shape[0]
     ids, gates = expert_ids.T, expert_gates.T
 
-    later = [out_weight.T, residual, norm_gain.reshape(1, -1), ids, gates, gate_weight, up_weight, down_weight]
+    later = [out_weight.T, residual, norm_gain.reshape(1, -1), ids, gates, down_weight]
     parts, *later = call(
         attend,
         [((seq * 2 * SLOTS, LANES), BF16)] + [(a.shape, a.dtype) for a in later],
@@ -253,33 +276,35 @@
             pltpu.SemaphoreType.DMA((len(later),)),
         ],
     )
-    weight, residual, gain, ids, gates, gate_weight, up_weight, down_weight = later
+    weight, residual, gain, ids, gates, down_weight = later
     parts = exchange(parts, "seq")
     (joined,) = call(combine, [((seq * SLOTS, LANES), BF16)], [parts])
     joined = exchange(joined, "seq")
-    (projected,) = call(
+    chosen, pick = call(
         project,
-        [((head, rows // 2, LANES), F32)],
-        [joined, weight],
+        [((head * seq * 2, LANES), BF16), ((seq * 2, 2 * rows), BF16)],
+        [joined, weight, residual, ids],
         scratch=[pltpu.VMEM((seq * SLOTS, LANES), F32)],
     )
-    summands = exchange(projected, "head")
-    after, chosen = call(
-        residual_step,
-        [(residual.shape, BF16), ((seq * 2, LANES), BF16)],
-        [summands, residual, ids],
-    )
-    chosen = exchange(chosen, "seq")
+    chosen = exchange(chosen, ("head", "seq"))
     (outputs,) = call(
         experts,
-        [((seq * head * 2, LANES), BF16)],
-        [chosen, gain, gate_weight, up_weight, down_weight, ids, gates],
-    )
-    outputs = exchange(outputs, ("seq", "head"))
-    (layer_out,) = call(
-        finish, [((rows, residual.shape[1] // head), BF16)], [outputs, after, ids], results=(0,)
-    )
-    return after, layer_out
+        [((head * seq * 2, LANES), BF16)],
+        [chosen, gain, down_weight, ids, gates, gate_weight, up_weight],
+        hbm=(5, 6),
+        scratch=[
+            pltpu.VMEM(gate_weight.shape[1:], BF16),
+            pltpu.VMEM(up_weight.shape[1:], BF16),
+            pltpu.SemaphoreType.DMA((2 * STREAMS,)),
+        ],
+    )
+    outputs = exchange(outputs, ("head", "seq"))
+    return call(
+        finish,
+        [(residual.shape, BF16), ((rows, residual.shape[1] // head), BF16)],
+        [outputs, pick, ids],
+        results=(0, 1),
+    )
 
 
 def solution(mesh):

time: 89.3 us -> 84 us (0.941)
  blocking collectives: 60.5 us -> 74.9 us
  waiting for transfers between devices: 12.3 us -> 0 us
  starting transfers between devices: 5.66 us -> 0 us
  Pallas kernels: 9.28 us -> 8.18 us
    all_to_all x4, blocking collectives: 60.5 us -> 74.9 us  [exchange(): return lax.all_to_all(x, axis, 0, 0, tiled=True)]
    all_to_all x1 -> x0, waiting for transfers between devices: 12.3 us -> none  [exchange(): return lax.all_to_all(x, axis, 0, 0, tiled=True)]
    all_to_all x1 -> x0, starting transfers between devices: 5.66 us -> none  [exchange(): return lax.all_to_all(x, axis, 0, 0, tiled=True)]
    pallas_call x6 -> x5, Pallas kernels: 9.28 us -> 8.18 us  [call(): pl.pallas_call(body, out_shape=[jax.ShapeDtypeStruct(shape, dtype) if i i...]
  transfers between devices with their start and end apart: 1 -> 0, of which waited for: 1 -> 0; matrix products, arithmetic and copies ran while one was open for 1% -> 0% of each run, Pallas kernels for 0% -> 0%
where the time goes in v2:
time: 84 us; the launch traced here: 83.8 us
  blocking collectives  74.9 us (89%)
  Pallas kernels  8.18 us (10%)
    all_to_all x4, blocking collectives, exchange(): return lax.all_to_all(x, axis, 0, 0, tiled=True)  74.9 us
    pallas_call x5, Pallas kernels, call(): pl.pallas_call(body, out_shape=[jax.ShapeDtypeStruct(shape, dtype) if i i...  8.18 us

profile of v2, /device:TPU:1, one launch (start us, length us, event | category | flops | bytes accessed | tf_op | source)
XLA Modules:
  0.0 83.8 jit_solution(14369441637321254247)
XLA Ops:
  0.6 2.5 %shard_map.131 = (bf16[512,128]{1,0:T(8,128)(2,1)S(1)}, bf16[64,2048]{1,0:T(8,128)(2,1)S(1)}, bf16[16,64]{1,0:T(8,128)(2,1)S(1)}, f32[1,4096]{1,0:T(1,128)S(1)},...) custom-call(s32[16]{0:T(128)} %lengths_hbm.1, bf16[16,2048]{1,0:T(8,128)(2,1)} %q_hbm.1, ...), custom_call_target="tpu_custom_call" | custom-call | tf_op jit(solution)/shard_map/pallas_call | solution.py:29
  3.1 24.1 %all_to_all.44 = bf16[64,8,128]{2,1,0:T(8,128)(2,1)S(1)} all-to-all(bf16[64,8,128]{2,1,0:T(8,128)(2,1)S(1)} %bitcast.18), channel_id=1, replica_groups=mesh['seq'=64,'head'=4] {'seq'}, dimensions={0} | all-to-all | bytes 262144 | tf_op jit(solution)/shard_map/all_to_all | solution.py:242
  27.2 0.3 shard_map.132
  27.5 13.9 %all_to_all.45 = bf16[64,4,128]{2,1,0:T(4,128)(2,1)S(1)} all-to-all(bf16[64,4,128]{2,1,0:T(4,128)(2,1)S(1)} %bitcast.16), channel_id=1, replica_groups=mesh['seq'=64,'head'=4] {'seq'}, dimensions={0} | all-to-all | bytes 131072 | tf_op jit(solution)/shard_map/all_to_all | solution.py:242
  41.4 0.4 shard_map.133
  41.8 18.8 %all_to_all.46 = bf16[256,2,128]{2,1,0:T(2,128)(2,1)S(1)} all-to-all(bf16[256,2,128]{2,1,0:T(2,128)(2,1)S(1)} %bitcast.19), channel_id=1, replica_groups=mesh['seq'=64,'head'=4] {'head','seq'}, dimensions={0} | all-to-all | bytes 262144 | tf_op jit(solution)/shard_map/all_to_all | solution.py:242
  60.6 3.8 %shard_map.134 = bf16[512,128]{1,0:T(8,128)(2,1)S(1)} custom-call(bf16[512,128]{1,0:T(8,128)(2,1)S(1)} %bitcast.12, f32[1,4096]{1,0:T(1,128)S(1)} %get-tuple-element.16.gain, bf16[1,384,4096]{2,1,0:T(8,128)(2,1)S(1)} %get-tuple-element.17.down, s32[8,16]{1,0:T(8,128)S(1)} %get-tuple-element.14.ids, f32[8,16]{1,0:T(8,128)S(1)} %get-tuple-element.18.gates, ...), custom_call_target="tpu_custom_call" | custom-call | tf_op jit(solution)/shard_map/pallas_call | solution.py:29
  64.5 18.2 %all_to_all.47 = bf16[256,2,128]{2,1,0:T(2,128)(2,1)S(1)} all-to-all(bf16[256,2,128]{2,1,0:T(2,128)(2,1)S(1)} %bitcast.13), channel_id=1, replica_groups=mesh['seq'=64,'head'=4] {'head','seq'}, dimensions={0} | all-to-all | bytes 262144 | tf_op jit(solution)/shard_map/all_to_all | solution.py:242
  82.6 1.2 %shard_map.135 = (bf16[16,64]{1,0:T(8,128)(2,1)}, bf16[16,16]{1,0:T(8,128)(2,1)}) custom-call(bf16[512,128]{1,0:T(8,128)(2,1)S(1)} %bitcast.14, bf16[128,32]{1,0:T(8,128)(2,1)S(1)} %get-tuple-element.19.pick, s32[8,16]{1,0:T(8,128)S(1)} %get-tuple-element.14.ids), custom_call_target="tpu_custom_call" | custom-call | tf_op jit(solution)/shard_map/pallas_call | solution.py:29

commit v3 on v2

v3 whole, which is shorter than its diff:
```python
import math

import jax
import jax.numpy as jnp
from jax import lax
from jax.experimental import pallas as pl
from jax.experimental.pallas import tpu as pltpu
from jax.sharding import PartitionSpec as P

HD = 128
LANES = 128
SLOTS = 4
MASKED = -1e30
F32 = jnp.float32
BF16 = jnp.bfloat16
NT = (((1,), (1,)), ((), ()))


def iota(shape, dim):
    return lax.broadcasted_iota(jnp.int32, shape, dim)


def call(body, outs, args, hbm=(), results=(), scratch=(), limit=16 << 20, cost=None):
    spaces = [pltpu.HBM if i in hbm else pltpu.VMEM for i in range(len(args))]
    args = [pltpu.with_memory_space_constraint(a, s) if s is pltpu.HBM else a for a, s in zip(args, spaces)]
    return pl.pallas_call(
        body,
        out_shape=[
            jax.ShapeDtypeStruct(shape, dtype) if i in results else pltpu.VMEM(shape, dtype)
            for i, (shape, dtype) in enumerate(outs)
        ],
        in_specs=[pl.BlockSpec(memory_space=s) for s in spaces],
        out_specs=[pl.BlockSpec(memory_space=pltpu.VMEM) for _ in outs],
        scratch_shapes=list(scratch),
        compiler_params=pltpu.CompilerParams(vmem_limit_bytes=limit),
        cost_estimate=cost,
    )(*args)


def attend(lengths_hbm, q_hbm, k_hbm, v_hbm, ids_hbm, gates_hbm, *refs):
    lengths, q, k, v, ids, gates, wide, sems = refs[-8:]
    later = (len(refs) - 12) // 2
    out, pick, turned, route = refs[2 * later : -8]
    rows, heads = q.shape[0], q.shape[1] // HD
    pairs = [(ids_hbm, ids), (gates_hbm, gates), (q_hbm, q), (k_hbm, k), (lengths_hbm, lengths), (v_hbm, v)]
    pairs += [(refs[i], refs[later + i]) for i in range(later)]
    fetch = [pltpu.make_async_copy(far, near, sems.at[i]) for i, (far, near) in enumerate(pairs)]
    for copy in fetch:
        copy.start()
    fetch[0].wait()
    fetch[1].wait()
    routing(ids[...], gates[...], pick, turned, route)
    fetch[2].wait()
    for h in range(heads):
        x = q[:, h * HD : (h + 1) * HD].astype(F32)
        at = (h // SLOTS) * 2 * SLOTS + h % SLOTS
        wide[pl.ds(at * rows, rows), :] = x
        wide[pl.ds((at + SLOTS) * rows, rows), :] = x
    tall = 2 * heads
    lane = iota((rows * tall, LANES), 1)
    upper = iota((rows * tall, LANES), 0) % (2 * SLOTS) < SLOTS
    fetch[3].wait()
    scores = [
        lax.dot_general(
            wide[pl.ds(r, tall, stride=rows), :].astype(BF16), k[r], NT, preferred_element_type=F32
        )
        for r in range(rows)
    ]
    scores = jnp.concatenate(scores, axis=0) * (1.0 / math.sqrt(HD))
    fetch[4].wait()
    place = lax.axis_index("seq") * k.shape[1] + iota((tall, k.shape[1]), 1)
    valid = jnp.concatenate([place < lengths[r] for r in range(rows)], axis=0)
    top = jnp.max(jnp.where(valid, scores, MASKED), axis=1, keepdims=True).astype(BF16).astype(F32)
    weights = jnp.where(valid, jnp.exp(scores - top), 0.0).astype(BF16)
    total = jnp.sum(weights.astype(F32), axis=1, keepdims=True)
    fetch[5].wait()
    numer = [
        jnp.dot(weights[r * tall : (r + 1) * tall], v[r], preferred_element_type=F32)
        for r in range(rows)
    ]
    high = total.astype(BF16).astype(F32)
    stats = jnp.where(lane < 64, top, jnp.where(lane < 96, high, total - high))
    out[...] = jnp.where(upper, jnp.concatenate(numer, axis=0), stats).astype(BF16)
    for copy in fetch[6:]:
        copy.wait()


def routing(ids, gates, pick, turned, route):
    chosen = selection(ids, pick.shape[0] // 2)
    pick[...] = chosen.astype(BF16)
    first = jnp.concatenate([ids[0:1, :], ids[0:1, :]], axis=1) == iota(chosen.shape, 0) // 2
    first = jnp.where(first, chosen, 0.0)
    both = jnp.concatenate([chosen, first, jnp.zeros((pick.shape[0], LANES - 2 * pick.shape[1]), F32)], axis=1)
    turned[...] = both.T[: turned.shape[0]].astype(BF16)

    rows = ids.shape[1]
    mine = ids == lax.axis_index("seq")
    gate = jnp.sum(jnp.where(mine, gates, 0.0), axis=0, keepdims=True)
    here = jnp.broadcast_to(jnp.max(mine.astype(F32), axis=0, keepdims=True), (8, rows))
    before = (iota((rows, rows), 0) < iota((rows, rows), 1)).astype(F32)
    rank = jnp.dot(here, before, preferred_element_type=F32)
    taken = (rank == iota((8, rows), 0).astype(F32)) & (here > 0.0)
    weight = jnp.sum(jnp.where(taken, gate, 0.0), axis=1, keepdims=True)
    route[...] = jnp.broadcast_to(weight, route.shape)


def combine(parts, out):
    count = parts.shape[0] // (2 * SLOTS)
    x = parts[...].astype(F32).reshape(count, 2 * SLOTS, LANES)
    numer, stats = x[:, :SLOTS], x[:, SLOTS:]
    top = stats[:, :, 0:1]
    total = stats[:, :, 64:65] + stats[:, :, 96:97]
    scale = jnp.exp(top - jnp.max(top, axis=0, keepdims=True))
    joined = jnp.sum(scale * numer, axis=0) / jnp.sum(scale * total, axis=0)
    pair = jnp.concatenate([joined, joined], axis=0)
    out[...] = jnp.broadcast_to(pair[None], (count // 2, 2 * SLOTS, LANES)).reshape(out.shape).astype(BF16)


def project(pieces, weight, residual, pick, out, wide):
    rows = residual.shape[0]
    heads = pieces.shape[0] // rows
    wide[...] = pieces[...].astype(F32)
    lhs = jnp.concatenate(
        [wide[pl.ds(h, rows, stride=heads), :].astype(BF16) for h in range(heads)], axis=1
    )
    part = lax.dot_general(lhs, weight[...], NT, preferred_element_type=F32)
    part = part + jnp.where(lax.axis_index("head") == 0, residual[...].astype(F32), 0.0)
    none = jnp.zeros_like(part)
    twice = jnp.concatenate(
        [jnp.concatenate([part, none], axis=1), jnp.concatenate([none, part], axis=1)], axis=0
    ).astype(BF16)
    send = jnp.dot(pick[...], twice, preferred_element_type=F32).astype(BF16)
    out[...] = jnp.concatenate([send] * (out.shape[0] // send.shape[0]), axis=0)


def selection(ids, count):
    top_k, rows = ids.shape
    shape = (count * 2, 2 * rows)
    expert = iota(shape, 0) // 2
    wide = jnp.concatenate([ids, ids], axis=1)
    hit = expert == wide[0:1, :]
    for k in range(1, top_k):
        hit = hit | (expert == wide[k : k + 1, :])
    hit = hit.astype(F32)
    square = (2 * rows, 2 * rows)
    before = (iota(square, 0) < iota(square, 1) % rows).astype(F32)
    rank = jnp.dot(hit, before, preferred_element_type=F32)
    slot = iota(shape, 0) % 2 + 2 * (iota(shape, 1) // rows)
    return jnp.where(rank == slot.astype(F32), hit, 0.0)


def swap(y):
    count = y.shape[0]
    row = iota(y.shape, 0) % 4
    lane = iota(y.shape, 1)
    z = pltpu.roll(y, 64, 1)
    up = pltpu.roll(z, count - 2, 0)
    down = pltpu.roll(z, 2, 0)
    return jnp.where(lane < 64, jnp.where(row < 2, y, down), jnp.where(row < 2, up, y))


def experts(pieces, gain, gate, up, down, route, out):
    width = gain.shape[1]
    blocks = width // LANES
    half = 2 * lax.axis_size("seq")
    heads = pieces.shape[0] // half
    summed = pieces[:half].astype(F32)
    for i in range(1, heads):
        summed = summed + pieces[i * half : (i + 1) * half].astype(F32)
    stacked = swap(summed).astype(BF16).astype(F32)
    tiles = []
    for b in range(blocks):
        tile = stacked[8 * (b // 2) : 8 * (b // 2) + 8]
        tiles.append(tile if b % 2 == 0 else pltpu.roll(tile, 4, 0))
    x = jnp.concatenate(tiles, axis=1)
    square = jnp.sum(x * x, axis=1, keepdims=True) * (1.0 / width)
    normed = (x * lax.rsqrt(square + 1e-6) * gain[...]).astype(BF16)
    gate_proj = jnp.dot(normed, gate[0], preferred_element_type=F32)
    up_proj = jnp.dot(normed, up[0], preferred_element_type=F32)
    hidden = (gate_proj / (1.0 + jnp.exp(-gate_proj)) * up_proj).astype(BF16)
    result = jnp.dot(hidden, down[0], preferred_element_type=F32) * route[:, 0:1]

    lower = iota((8, LANES), 0) < 4
    pairs = []
    for b in range(0, blocks, 2):
        left = result[:, b * LANES : (b + 1) * LANES]
        right = result[:, (b + 1) * LANES : (b + 2) * LANES]
        pairs.append(jnp.where(lower, left, pltpu.roll(right, 4, 0)))
    mixed = jnp.concatenate(pairs, axis=0)
    head = lax.axis_index("head")
    group = iota(mixed.shape, 1) // 16 % heads
    moved = pltpu.roll(stacked, jnp.where(head % 2 == 0, 16, LANES - 16), 1)
    for target in range(heads):
        carried = jnp.where(target == head, moved, stacked)
        packed = swap(jnp.where(group == target, mixed, carried))
        out[pl.ds(target * half, half), :] = packed.astype(BF16)


def finish(pieces, turned, after, out):
    half = turned.shape[1]
    rows, width = out.shape
    heads = pieces.shape[0] // half
    head = lax.axis_index("head")
    group = iota((rows, LANES), 1) // 16
    mixture = jnp.zeros((rows, LANES), F32)
    own = jnp.zeros((rows, LANES), F32)
    for source in range(heads):
        got = jnp.dot(turned[...], pieces[source * half : (source + 1) * half], preferred_element_type=F32)
        mixture = mixture + got[:rows] + pltpu.roll(got[rows : 2 * rows], 64, 1)
        carried = got[2 * rows : 3 * rows] + pltpu.roll(got[3 * rows :], 64, 1)
        moved = pltpu.roll(carried, LANES - 16 if source % 2 == 0 else 16, 1)
        own = own + jnp.where(group == source, jnp.where(head == source, moved, carried), 0.0)
    after[...] = own[:, : after.shape[1]].astype(BF16)
    shift = (LANES - width * head) % LANES
    out[...] = pltpu.roll(mixture + own, shift, 1)[:, :width].astype(BF16)


def exchange(x, axis):
    return lax.all_to_all(x, axis, 0, 0, tiled=True)


def local(
    queries,
    keys,
    values,
    lengths,
    residual,
    out_weight,
    norm_gain,
    expert_ids,
    expert_gates,
    gate_weight,
    up_weight,
    down_weight,
):
    seq, head = lax.axis_size("seq"), lax.axis_size("head")
    rows = queries.shape[0]
    later = [out_weight.T, residual, norm_gain.reshape(1, -1)]
    weight, residual, gain, parts, pick, turned, route = call(
        attend,
        [(a.shape, a.dtype) for a in later]
        + [((seq * 2 * SLOTS, LANES), BF16)]
        + [((seq * 2, 2 * rows), BF16), ((4 * rows, seq * 2), BF16), ((8, LANES), F32)],
        [lengths, queries, keys, values, expert_ids.T, expert_gates.T, *later],
        hbm=range(6 + len(later)),
        scratch=[
            pltpu.SMEM(lengths.shape, lengths.dtype),
            pltpu.VMEM(queries.shape, BF16),
            pltpu.VMEM(keys.shape, BF16),
            pltpu.VMEM(values.shape, BF16),
            pltpu.VMEM(expert_ids.shape[::-1], expert_ids.dtype),
            pltpu.VMEM(expert_gates.shape[::-1], F32),
            pltpu.VMEM((2 * queries.shape[1] // HD * rows, HD), F32),
            pltpu.SemaphoreType.DMA((6 + len(later),)),
        ],
    )
    parts = exchange(parts, "seq")
    cost = pl.CostEstimate(flops=1 << 33, bytes_accessed=1 << 25, transcendentals=0)
    (joined,) = call(combine, [((seq * SLOTS, LANES), BF16)], [parts], cost=cost)
    joined = exchange(joined, "seq")
    (chosen,) = call(
        project,
        [((head * seq * 2, LANES), BF16)],
        [joined, weight, residual, pick],
        scratch=[pltpu.VMEM((seq * SLOTS, LANES), F32)],
        cost=cost,
    )
    chosen = exchange(chosen, ("head", "seq"))
    (outputs,) = call(
        experts,
        [((head * seq * 2, LANES), BF16)],
        [chosen, gain, gate_weight, up_weight, down_weight, route],
    )
    outputs = exchange(outputs, ("head", "seq"))
    return call(
        finish,
        [(residual.shape, BF16), ((rows, residual.shape[1] // head), BF16)],
        [outputs, turned],
        results=(0, 1),
    )


def solution(mesh):
    in_specs = (
        P(None, "head"),
        P(None, "seq", "head"),
        P(None, "seq", "head"),
        P(),
        P(None, "seq"),
        P("head", "seq"),
        P(),
        P(),
        P(),
        P("seq", None, "head"),
        P("seq", None, "head"),
        P("seq", "head", None),
    )
    out_specs = (P(None, "seq"), P(None, ("seq", "head")))
    return jax.shard_map(local, mesh=mesh, in_specs=in_specs, out_specs=out_specs, check_vma=False)
```

time: 84 us -> 81.3 us (0.968)
  Pallas kernels: 8.18 us -> 5.47 us
    pallas_call x5, Pallas kernels: 8.18 us -> 5.47 us  [call(): pl.pallas_call(body, out_shape=[jax.ShapeDtypeStruct(shape, dtype) if i i...]
where the time goes in v3:
time: 81.3 us; the launch traced here: 81.1 us
  blocking collectives  74.9 us (92%)
  Pallas kernels  5.47 us (7%)
    all_to_all x4, blocking collectives, exchange(): return lax.all_to_all(x, axis, 0, 0, tiled=True)  74.9 us
    pallas_call x5, Pallas kernels, call(): pl.pallas_call(body, out_shape=[jax.ShapeDtypeStruct(shape, dtype) if i i...  5.47 us

profile of v3, /device:TPU:1, one launch (start us, length us, event | category | flops | bytes accessed | tf_op | source)
XLA Modules:
  0.0 81.1 jit_solution(2781635596981248459)
XLA Ops:
  0.6 2.1 %shard_map.131 = (bf16[64,2048]{1,0:T(8,128)(2,1)S(1)}, bf16[16,64]{1,0:T(8,128)(2,1)S(1)}, f32[1,4096]{1,0:T(1,128)S(1)}, bf16[512,128]{1,0:T(8,128)(2,1)S(1)},...) custom-call(s32[16]{0:T(128)} %lengths_hbm.1, bf16[16,2048]{1,0:T(8,128)(2,1)} %q_hbm.1, ...), custom_call_target="tpu_custom_call" | custom-call | tf_op jit(solution)/shard_map/pallas_call | solution.py:26
  2.7 24.1 %all_to_all.44 = bf16[64,8,128]{2,1,0:T(8,128)(2,1)S(1)} all-to-all(bf16[64,8,128]{2,1,0:T(8,128)(2,1)S(1)} %bitcast.15), channel_id=1, replica_groups=mesh['seq'=64,'head'=4] {'seq'}, dimensions={0} | all-to-all | bytes 262144 | tf_op jit(solution)/shard_map/all_to_all | solution.py:219
  26.8 0.3 shard_map.132
  27.1 13.9 %all_to_all.45 = bf16[64,4,128]{2,1,0:T(4,128)(2,1)S(1)} all-to-all(bf16[64,4,128]{2,1,0:T(4,128)(2,1)S(1)} %bitcast.19), channel_id=1, replica_groups=mesh['seq'=64,'head'=4] {'seq'}, dimensions={0} | all-to-all | bytes 131072 | tf_op jit(solution)/shard_map/all_to_all | solution.py:219
  41.0 0.0 copy-start
  41.0 0.0 copy-start.1
  41.0 0.0 copy-start.2
  41.0 0.4 shard_map.133
  41.4 18.8 %all_to_all.46 = bf16[256,2,128]{2,1,0:T(2,128)(2,1)S(1)} all-to-all(bf16[256,2,128]{2,1,0:T(2,128)(2,1)S(1)} %bitcast.16), channel_id=1, replica_groups=mesh['seq'=64,'head'=4] {'head','seq'}, dimensions={0} | all-to-all | bytes 262144 | tf_op jit(solution)/shard_map/all_to_all | solution.py:219
  60.2 0.0 copy-done
  60.2 0.0 copy-done.1
  60.2 0.0 copy-done.2
  60.2 1.7 %shard_map.134 = bf16[512,128]{1,0:T(8,128)(2,1)S(1)} custom-call(bf16[512,128]{1,0:T(8,128)(2,1)S(1)} %bitcast.12, f32[1,4096]{1,0:T(1,128)S(1)} %get-tuple-element.13.gain, bf16[1,4096,384]{2,1,0:T(8,128)(2,1)S(1)} %copy-done, bf16[1,4096,384]{2,1,0:T(8,128)(2,1)S(1)} %copy-done.1, bf16[1,384,4096]{2,1,0:T(8,128)(2,1)S(1)} %copy-done.2, ...), custom_call_target="tpu_custom_call" | custom-call | tf_op jit(solution)/shard_map/pallas_call | solution.py:26
  61.9 18.2 %all_to_all.47 = bf16[256,2,128]{2,1,0:T(2,128)(2,1)S(1)} all-to-all(bf16[256,2,128]{2,1,0:T(2,128)(2,1)S(1)} %bitcast.13), channel_id=1, replica_groups=mesh['seq'=64,'head'=4] {'head','seq'}, dimensions={0} | all-to-all | bytes 262144 | tf_op jit(solution)/shard_map/all_to_all | solution.py:219
  80.1 1.0 %shard_map.135 = (bf16[16,64]{1,0:T(8,128)(2,1)}, bf16[16,16]{1,0:T(8,128)(2,1)}) custom-call(bf16[512,128]{1,0:T(8,128)(2,1)S(1)} %bitcast.14, bf16[64,128]{1,0:T(8,128)(2,1)S(1)} %get-tuple-element.15.turned), custom_call_target="tpu_custom_call" | custom-call | tf_op jit(solution)/shard_map/pallas_call | solution.py:26
Async XLA Ops:
  41.0 19.2 %copy-start = (bf16[1,4096,384]{2,1,0:T(8,128)(2,1)S(1)}, bf16[1,4096,384]{2,1,0:T(8,128)(2,1)}, u32[]{:S(2)}) copy-start(bf16[1,4096,384]{2,1,0:T(8,128)(2,1)} %gate.1) | copy-start | bytes 9437188
  41.0 19.2 %copy-start.1 = (bf16[1,4096,384]{2,1,0:T(8,128)(2,1)S(1)}, bf16[1,4096,384]{2,1,0:T(8,128)(2,1)}, u32[]{:S(2)}) copy-start(bf16[1,4096,384]{2,1,0:T(8,128)(2,1)} %up.1) | copy-start | bytes 9437188
  41.0 19.2 %copy-start.2 = (bf16[1,384,4096]{2,1,0:T(8,128)(2,1)S(1)}, bf16[1,384,4096]{2,1,0:T(8,128)(2,1)}, u32[]{:S(2)}) copy-start(bf16[1,384,4096]{2,1,0:T(8,128)(2,1)} %down.1) | copy-start | bytes 9437188

commit v4 on v3

--- a/solution.py
+++ b/solution.py
@@ -5,11 +5,14 @@
 from jax import lax
 from jax.experimental import pallas as pl
 from jax.experimental.pallas import tpu as pltpu
+from jax.sharding import Mesh
 from jax.sharding import PartitionSpec as P
 
 HD = 128
 LANES = 128
-SLOTS = 4
+NEAR = 8
+PAIRS = 32
+PIECE = PAIRS + PAIRS // 4
 MASKED = -1e30
 F32 = jnp.float32
 BF16 = jnp.bfloat16
@@ -52,35 +55,27 @@
     routing(ids[...], gates[...], pick, turned, route)
     fetch[2].wait()
     for h in range(heads):
-        x = q[:, h * HD : (h + 1) * HD].astype(F32)
-        at = (h // SLOTS) * 2 * SLOTS + h % SLOTS
-        wide[pl.ds(at * rows, rows), :] = x
-        wide[pl.ds((at + SLOTS) * rows, rows), :] = x
-    tall = 2 * heads
-    lane = iota((rows * tall, LANES), 1)
-    upper = iota((rows * tall, LANES), 0) % (2 * SLOTS) < SLOTS
+        wide[pl.ds(h * rows, rows), :] = q[:, h * HD : (h + 1) * HD].astype(F32)
     fetch[3].wait()
     scores = [
         lax.dot_general(
-            wide[pl.ds(r, tall, stride=rows), :].astype(BF16), k[r], NT, preferred_element_type=F32
+            wide[pl.ds(r, heads, stride=rows), :].astype(BF16), k[r], NT, preferred_element_type=F32
         )
         for r in range(rows)
     ]
     scores = jnp.concatenate(scores, axis=0) * (1.0 / math.sqrt(HD))
     fetch[4].wait()
-    place = lax.axis_index("seq") * k.shape[1] + iota((tall, k.shape[1]), 1)
+    place = own_block() * k.shape[1] + iota((heads, k.shape[1]), 1)
     valid = jnp.concatenate([place < lengths[r] for r in range(rows)], axis=0)
     top = jnp.max(jnp.where(valid, scores, MASKED), axis=1, keepdims=True).astype(BF16).astype(F32)
     weights = jnp.where(valid, jnp.exp(scores - top), 0.0).astype(BF16)
     total = jnp.sum(weights.astype(F32), axis=1, keepdims=True)
     fetch[5].wait()
     numer = [
-        jnp.dot(weights[r * tall : (r + 1) * tall], v[r], preferred_element_type=F32)
+        jnp.dot(weights[r * heads : (r + 1) * heads], v[r], preferred_element_type=F32)
         for r in range(rows)
     ]
-    high = total.astype(BF16).astype(F32)
-    stats = jnp.where(lane < 64, top, jnp.where(lane < 96, high, total - high))
-    out[...] = jnp.where(upper, jnp.concatenate(numer, axis=0), stats).astype(BF16)
+    out[...] = joint(jnp.concatenate(numer, axis=0), top, total, out.shape[0] // PIECE)
     for copy in fetch[6:]:
         copy.wait()
 
@@ -94,7 +89,7 @@
     turned[...] = both.T[: turned.shape[0]].astype(BF16)
 
     rows = ids.shape[1]
-    mine = ids == lax.axis_index("seq")
+    mine = ids == own_block()
     gate = jnp.sum(jnp.where(mine, gates, 0.0), axis=0, keepdims=True)
     here = jnp.broadcast_to(jnp.max(mine.astype(F32), axis=0, keepdims=True), (8, rows))
     before = (iota((rows, rows), 0) < iota((rows, rows), 1)).astype(F32)
@@ -104,16 +99,59 @@
     route[...] = jnp.broadcast_to(weight, route.shape)
 
 
+def own_block():
+    return lax.axis_index("far") * lax.axis_size("near") + lax.axis_index("near")
+
+
+def joint(numer, top, total, count):
+    pairs = numer.shape[0]
+    lane, row = iota(numer.shape, 1), iota(numer.shape, 0)
+    high = total.astype(BF16).astype(F32)
+    part = lane % 32
+    stats = jnp.where(part < 16, top, jnp.where(part < 24, high, total - high))
+    stats = jnp.where(lane // 32 == row % 4, stats, 0.0).astype(BF16)
+    gather = (iota((pairs // 4, pairs), 0) == iota((pairs // 4, pairs), 1) // 4).astype(BF16)
+    packed = jnp.dot(gather, stats, preferred_element_type=F32)
+    pieces = []
+    for i in range(count):
+        pieces += [numer[i * PAIRS : (i + 1) * PAIRS], packed[i * PAIRS // 4 : (i + 1) * PAIRS // 4]]
+    return jnp.concatenate(pieces, axis=0).astype(BF16)
+
+
+def merged(pieces):
+    count = pieces.shape[0] // PIECE
+    wide = pieces.astype(F32)
+    parts = [wide[i * PIECE : (i + 1) * PIECE] for i in range(count)]
+    numer = [part[:PAIRS] for part in parts]
+    packed = jnp.concatenate([part[PAIRS:] for part in parts], axis=0).astype(BF16)
+    pairs = count * PAIRS
+    spread = (iota((pairs, pairs // 4), 0) // 4 == iota((pairs, pairs // 4), 1)).astype(BF16)
+    stats = jnp.dot(spread, packed, preferred_element_type=F32)
+    at = iota(stats.shape, 1) - 32 * (iota(stats.shape, 0) % 4)
+    ones = jnp.ones((LANES, LANES), BF16)
+    tops = jnp.dot(jnp.where(at == 0, stats, 0.0).astype(BF16), ones, preferred_element_type=F32)
+    sums = jnp.where((at == 16) | (at == 24), stats, 0.0).astype(BF16)
+    sums = jnp.dot(sums, ones, preferred_element_type=F32)
+    top = tops[:PAIRS]
+    for i in range(1, count):
+        top = jnp.maximum(top, tops[i * PAIRS : (i + 1) * PAIRS])
+    numers = totals = jnp.zeros((PAIRS, LANES), F32)
+    for i in range(count):
+        scale = jnp.exp(tops[i * PAIRS : (i + 1) * PAIRS] - top)
+        numers = numers + scale * numer[i]
+        totals = totals + scale * sums[i * PAIRS : (i + 1) * PAIRS]
+    return numers, top, totals
+
+
 def combine(parts, out):
-    count = parts.shape[0] // (2 * SLOTS)
-    x = parts[...].astype(F32).reshape(count, 2 * SLOTS, LANES)
-    numer, stats = x[:, :SLOTS], x[:, SLOTS:]
-    top = stats[:, :, 0:1]
-    total = stats[:, :, 64:65] + stats[:, :, 96:97]
-    scale = jnp.exp(top - jnp.max(top, axis=0, keepdims=True))
-    joined = jnp.sum(scale * numer, axis=0) / jnp.sum(scale * total, axis=0)
-    pair = jnp.concatenate([joined, joined], axis=0)
-    out[...] = jnp.broadcast_to(pair[None], (count // 2, 2 * SLOTS, LANES)).reshape(out.shape).astype(BF16)
+    numer, top, total = merged(parts[...])
+    piece = joint(numer, top, total, 1)
+    out[...] = jnp.concatenate([piece.astype(F32)] * (out.shape[0] // PIECE), axis=0).astype(BF16)
+
+
+def complete(parts, out):
+    numer, _, total = merged(parts[...])
+    out[...] = jnp.concatenate([(numer / total).astype(BF16)] * (out.shape[0] // PAIRS), axis=0)
 
 
 def project(pieces, weight, residual, pick, out, wide):
@@ -162,7 +200,7 @@
 def experts(pieces, gain, gate, up, down, route, out):
     width = gain.shape[1]
     blocks = width // LANES
-    half = 2 * lax.axis_size("seq")
+    half = 2 * lax.axis_size("far") * lax.axis_size("near")
     heads = pieces.shape[0] // half
     summed = pieces[:half].astype(F32)
     for i in range(1, heads):
@@ -233,13 +271,14 @@
     up_weight,
     down_weight,
 ):
-    seq, head = lax.axis_size("seq"), lax.axis_size("head")
+    far, near, head = lax.axis_size("far"), lax.axis_size("near"), lax.axis_size("head")
+    seq = far * near
     rows = queries.shape[0]
     later = [out_weight.T, residual, norm_gain.reshape(1, -1)]
     weight, residual, gain, parts, pick, turned, route = call(
         attend,
         [(a.shape, a.dtype) for a in later]
-        + [((seq * 2 * SLOTS, LANES), BF16)]
+        + [((near * PIECE, LANES), BF16)]
         + [((seq * 2, 2 * rows), BF16), ((4 * rows, seq * 2), BF16), ((8, LANES), F32)],
         [lengths, queries, keys, values, expert_ids.T, expert_gates.T, *later],
         hbm=range(6 + len(later)),
@@ -250,28 +289,30 @@
             pltpu.VMEM(values.shape, BF16),
             pltpu.VMEM(expert_ids.shape[::-1], expert_ids.dtype),
             pltpu.VMEM(expert_gates.shape[::-1], F32),
-            pltpu.VMEM((2 * queries.shape[1] // HD * rows, HD), F32),
+            pltpu.VMEM((queries.shape[1] // HD * rows, HD), F32),
             pltpu.SemaphoreType.DMA((6 + len(later),)),
         ],
     )
-    parts = exchange(parts, "seq")
+    parts = exchange(parts, "near")
     cost = pl.CostEstimate(flops=1 << 33, bytes_accessed=1 << 25, transcendentals=0)
-    (joined,) = call(combine, [((seq * SLOTS, LANES), BF16)], [parts], cost=cost)
-    joined = exchange(joined, "seq")
+    (parts,) = call(combine, [((far * PIECE, LANES), BF16)], [parts], cost=cost)
+    parts = exchange(parts, "far")
+    (joined,) = call(complete, [((near * PAIRS, LANES), BF16)], [parts], cost=cost)
+    joined = exchange(joined, "near")
     (chosen,) = call(
         project,
         [((head * seq * 2, LANES), BF16)],
         [joined, weight, residual, pick],
-        scratch=[pltpu.VMEM((seq * SLOTS, LANES), F32)],
+        scratch=[pltpu.VMEM((near * PAIRS, LANES), F32)],
         cost=cost,
     )
-    chosen = exchange(chosen, ("head", "seq"))
+    chosen = exchange(chosen, ("head", "far", "near"))
     (outputs,) = call(
         experts,
         [((head * seq * 2, LANES), BF16)],
         [chosen, gain, gate_weight, up_weight, down_weight, route],
     )
-    outputs = exchange(outputs, ("head", "seq"))
+    outputs = exchange(outputs, ("head", "far", "near"))
     return call(
         finish,
         [(residual.shape, BF16), ((rows, residual.shape[1] // head), BF16)],
@@ -281,19 +322,22 @@
 
 
 def solution(mesh):
+    seq, head = mesh.shape["seq"], mesh.shape["head"]
+    mesh = Mesh(mesh.devices.reshape(seq // NEAR, NEAR, head), ("far", "near", "head"))
+    seq = ("far", "near")
     in_specs = (
         P(None, "head"),
-        P(None, "seq", "head"),
-        P(None, "seq", "head"),
+        P(None, seq, "head"),
+        P(None, seq, "head"),
         P(),
-        P(None, "seq"),
-        P("head", "seq"),
+        P(None, seq),
+        P("head", seq),
         P(),
         P(),
         P(),
-        P("seq", None, "head"),
-        P("seq", None, "head"),
-        P("seq", "head", None),
-    )
-    out_specs = (P(None, "seq"), P(None, ("seq", "head")))
+        P(seq, None, "head"),
+        P(seq, None, "head"),
+        P(seq, "head", None),
+    )
+    out_specs = (P(None, seq), P(None, (*seq, "head")))
     return jax.shard_map(local, mesh=mesh, in_specs=in_specs, out_specs=out_specs, check_vma=False)

time: 81.3 us -> 79.5 us (0.978)
  blocking collectives: 74.9 us -> 72.6 us
    all_to_all x4 -> x5, blocking collectives: 74.9 us -> 72.6 us  [exchange(): return lax.all_to_all(x, axis, 0, 0, tiled=True)]
    pallas_call x5 -> x6, Pallas kernels: 5.47 us -> 5.92 us  [call(): pl.pallas_call(body, out_shape=[jax.ShapeDtypeStruct(shape, dtype) if i i...]
where the time goes in v4:
time: 79.5 us; the launch traced here: 79.2 us
  blocking collectives  72.6 us (91%)
  Pallas kernels  5.92 us (7%)
    all_to_all x5, blocking collectives, exchange(): return lax.all_to_all(x, axis, 0, 0, tiled=True)  72.6 us
    pallas_call x6, Pallas kernels, call(): pl.pallas_call(body, out_shape=[jax.ShapeDtypeStruct(shape, dtype) if i i...  5.92 us

profile of v4, /device:TPU:1, one launch (start us, length us, event | category | flops | bytes accessed | tf_op | source)
XLA Modules:
  0.0 79.2 jit_solution(7398444610310751561)
XLA Ops:
  0.6 2.1 %shard_map.131 = (bf16[64,2048]{1,0:T(8,128)(2,1)S(1)}, bf16[16,64]{1,0:T(8,128)(2,1)S(1)}, f32[1,4096]{1,0:T(1,128)S(1)}, bf16[320,128]{1,0:T(8,128)(2,1)S(1)},...) custom-call(s32[16]{0:T(128)} %lengths_hbm.1, bf16[16,2048]{1,0:T(8,128)(2,1)} %q_hbm.1, ...), custom_call_target="tpu_custom_call" | custom-call | tf_op jit(solution)/shard_map/pallas_call | solution.py:29
  2.7 10.7 %all_to_all.55 = bf16[8,40,128]{2,1,0:T(8,128)(2,1)S(1)} all-to-all(bf16[8,40,128]{2,1,0:T(8,128)(2,1)S(1)} %bitcast.18), channel_id=1, replica_groups=mesh['far'=8,'near'=8,'head'=4] {'near'}, dimensions={0} | all-to-all | bytes 163840 | tf_op jit(solution)/shard_map/all_to_all | solution.py:257
  13.4 0.4 shard_map.132
  13.8 15.5 %all_to_all.56 = bf16[8,40,128]{2,1,0:T(8,128)(2,1)S(1)} all-to-all(bf16[8,40,128]{2,1,0:T(8,128)(2,1)S(1)} %bitcast.20), channel_id=1, replica_groups=mesh['far'=8,'near'=8,'head'=4] {'far'}, dimensions={0} | all-to-all | bytes 163840 | tf_op jit(solution)/shard_map/all_to_all | solution.py:257
  29.3 0.3 shard_map.133
  29.6 9.3 %all_to_all.57 = bf16[8,32,128]{2,1,0:T(8,128)(2,1)S(1)} all-to-all(bf16[8,32,128]{2,1,0:T(8,128)(2,1)S(1)} %bitcast.23), channel_id=1, replica_groups=mesh['far'=8,'near'=8,'head'=4] {'near'}, dimensions={0} | all-to-all | bytes 131072 | tf_op jit(solution)/shard_map/all_to_all | solution.py:257
  39.0 0.0 copy-start
  39.0 0.0 copy-start.1
  39.0 0.0 copy-start.2
  39.0 0.4 shard_map.134
  39.4 18.9 %all_to_all.58 = bf16[256,2,128]{2,1,0:T(2,128)(2,1)S(1)} all-to-all(bf16[256,2,128]{2,1,0:T(2,128)(2,1)S(1)} %bitcast.17), channel_id=1, replica_groups=mesh['far'=8,'near'=8,'head'=4] {'head','far','near'}, dimensions={0} | all-to-all | bytes 262144 | tf_op jit(solution)/shard_map/all_to_all | solution.py:257
  58.4 0.0 copy-done
  58.4 0.0 copy-done.1
  58.4 0.0 copy-done.2
  58.4 1.7 %shard_map.135 = bf16[512,128]{1,0:T(8,128)(2,1)S(1)} custom-call(bf16[512,128]{1,0:T(8,128)(2,1)S(1)} %bitcast.14, f32[1,4096]{1,0:T(1,128)S(1)} %get-tuple-element.13.gain, bf16[1,4096,384]{2,1,0:T(8,128)(2,1)S(1)} %copy-done, bf16[1,4096,384]{2,1,0:T(8,128)(2,1)S(1)} %copy-done.1, bf16[1,384,4096]{2,1,0:T(8,128)(2,1)S(1)} %copy-done.2, ...), custom_call_target="tpu_custom_call" | custom-call | tf_op jit(solution)/shard_map/pallas_call | solution.py:29
  60.1 18.2 %all_to_all.59 = bf16[256,2,128]{2,1,0:T(2,128)(2,1)S(1)} all-to-all(bf16[256,2,128]{2,1,0:T(2,128)(2,1)S(1)} %bitcast.15), channel_id=1, replica_groups=mesh['far'=8,'near'=8,'head'=4] {'head','far','near'}, dimensions={0} | all-to-all | bytes 262144 | tf_op jit(solution)/shard_map/all_to_all | solution.py:257
  78.2 1.0 %shard_map.136 = (bf16[16,64]{1,0:T(8,128)(2,1)}, bf16[16,16]{1,0:T(8,128)(2,1)}) custom-call(bf16[512,128]{1,0:T(8,128)(2,1)S(1)} %bitcast.16, bf16[64,128]{1,0:T(8,128)(2,1)S(1)} %get-tuple-element.15.turned), custom_call_target="tpu_custom_call" | custom-call | tf_op jit(solution)/shard_map/pallas_call | solution.py:29
Async XLA Ops:
  39.0 19.4 %copy-start = (bf16[1,4096,384]{2,1,0:T(8,128)(2,1)S(1)}, bf16[1,4096,384]{2,1,0:T(8,128)(2,1)}, u32[]{:S(2)}) copy-start(bf16[1,4096,384]{2,1,0:T(8,128)(2,1)} %gate.1) | copy-start | bytes 9437188
  39.0 19.4 %copy-start.1 = (bf16[1,4096,384]{2,1,0:T(8,128)(2,1)S(1)}, bf16[1,4096,384]{2,1,0:T(8,128)(2,1)}, u32[]{:S(2)}) copy-start(bf16[1,4096,384]{2,1,0:T(8,128)(2,1)} %up.1) | copy-start | bytes 9437188
  39.0 19.4 %copy-start.2 = (bf16[1,384,4096]{2,1,0:T(8,128)(2,1)S(1)}, bf16[1,384,4096]{2,1,0:T(8,128)(2,1)}, u32[]{:S(2)}) copy-start(bf16[1,384,4096]{2,1,0:T(8,128)(2,1)} %down.1) | copy-start | bytes 9437188

commit v5 on v4

--- a/solution.py
+++ b/solution.py
@@ -104,54 +104,53 @@
 
 
 def joint(numer, top, total, count):
-    pairs = numer.shape[0]
-    lane, row = iota(numer.shape, 1), iota(numer.shape, 0)
+    lane = iota(numer.shape, 1)
     high = total.astype(BF16).astype(F32)
     part = lane % 32
     stats = jnp.where(part < 16, top, jnp.where(part < 24, high, total - high))
-    stats = jnp.where(lane // 32 == row % 4, stats, 0.0).astype(BF16)
-    gather = (iota((pairs // 4, pairs), 0) == iota((pairs // 4, pairs), 1) // 4).astype(BF16)
-    packed = jnp.dot(gather, stats, preferred_element_type=F32)
+    lane = iota((8, LANES), 1)
     pieces = []
     for i in range(count):
-        pieces += [numer[i * PAIRS : (i + 1) * PAIRS], packed[i * PAIRS // 4 : (i + 1) * PAIRS // 4]]
+        quarters = [stats[i * PAIRS + 8 * a : i * PAIRS + 8 * a + 8] for a in range(PAIRS // 8)]
+        packed = quarters[-1]
+        for a in range(PAIRS // 8 - 1):
+            packed = jnp.where(lane // 32 == a, quarters[a], packed)
+        pieces += [numer[i * PAIRS : (i + 1) * PAIRS], packed]
     return jnp.concatenate(pieces, axis=0).astype(BF16)
 
 
 def merged(pieces):
-    count = pieces.shape[0] // PIECE
     wide = pieces.astype(F32)
-    parts = [wide[i * PIECE : (i + 1) * PIECE] for i in range(count)]
-    numer = [part[:PAIRS] for part in parts]
-    packed = jnp.concatenate([part[PAIRS:] for part in parts], axis=0).astype(BF16)
-    pairs = count * PAIRS
-    spread = (iota((pairs, pairs // 4), 0) // 4 == iota((pairs, pairs // 4), 1)).astype(BF16)
-    stats = jnp.dot(spread, packed, preferred_element_type=F32)
-    at = iota(stats.shape, 1) - 32 * (iota(stats.shape, 0) % 4)
-    ones = jnp.ones((LANES, LANES), BF16)
-    tops = jnp.dot(jnp.where(at == 0, stats, 0.0).astype(BF16), ones, preferred_element_type=F32)
-    sums = jnp.where((at == 16) | (at == 24), stats, 0.0).astype(BF16)
-    sums = jnp.dot(sums, ones, preferred_element_type=F32)
-    top = tops[:PAIRS]
-    for i in range(1, count):
-        top = jnp.maximum(top, tops[i * PAIRS : (i + 1) * PAIRS])
-    numers = totals = jnp.zeros((PAIRS, LANES), F32)
-    for i in range(count):
-        scale = jnp.exp(tops[i * PAIRS : (i + 1) * PAIRS] - top)
-        numers = numers + scale * numer[i]
-        totals = totals + scale * sums[i * PAIRS : (i + 1) * PAIRS]
-    return numers, top, totals
+    parts = [wide[i : i + PIECE] for i in range(0, pieces.shape[0], PIECE)]
+    packed = [part[PAIRS:] for part in parts]
+    top = packed[0]
+    for one in packed[1:]:
+        top = jnp.maximum(top, one)
+    numers, totals = jnp.zeros((PAIRS, LANES), F32), jnp.zeros((8, LANES), F32)
+    for part, one in zip(parts, packed):
+        scale = jnp.exp(one - top)
+        totals = totals + pltpu.roll(scale, 16, 1) * one
+        column = jnp.concatenate(
+            [jnp.broadcast_to(scale[:, a : a + 1], (8, LANES)) for a in range(0, LANES, 32)], axis=0
+        )
+        numers = numers + column * part[:PAIRS]
+    return numers, top, totals + pltpu.roll(totals, LANES - 8, 1)
 
 
 def combine(parts, out):
     numer, top, total = merged(parts[...])
-    piece = joint(numer, top, total, 1)
-    out[...] = jnp.concatenate([piece.astype(F32)] * (out.shape[0] // PIECE), axis=0).astype(BF16)
+    part = iota(top.shape, 1) % 32
+    high = total.astype(BF16).astype(F32)
+    packed = jnp.where(part < 16, top, jnp.where(part < 24, high, pltpu.roll(total - high, 8, 1)))
+    out[...] = jnp.concatenate([numer, packed] * (out.shape[0] // PIECE), axis=0).astype(BF16)
 
 
 def complete(parts, out):
     numer, _, total = merged(parts[...])
-    out[...] = jnp.concatenate([(numer / total).astype(BF16)] * (out.shape[0] // PAIRS), axis=0)
+    column = jnp.concatenate(
+        [jnp.broadcast_to(total[:, a : a + 1], (8, LANES)) for a in range(16, LANES, 32)], axis=0
+    )
+    out[...] = jnp.concatenate([(numer / column).astype(BF16)] * (out.shape[0] // PAIRS), axis=0)
 
 
 def project(pieces, weight, residual, pick, out, wide):
@@ -239,15 +238,20 @@
     rows, width = out.shape
     heads = pieces.shape[0] // half
     head = lax.axis_index("head")
-    group = iota((rows, LANES), 1) // 16
-    mixture = jnp.zeros((rows, LANES), F32)
-    own = jnp.zeros((rows, LANES), F32)
+    group = iota((rows, LANES), 1) // 16 % heads
+    none = jnp.zeros((rows, LANES), F32)
+    mixture, own, beside = [none, none], [none, none], [none, none]
     for source in range(heads):
         got = jnp.dot(turned[...], pieces[source * half : (source + 1) * half], preferred_element_type=F32)
-        mixture = mixture + got[:rows] + pltpu.roll(got[rows : 2 * rows], 64, 1)
-        carried = got[2 * rows : 3 * rows] + pltpu.roll(got[3 * rows :], 64, 1)
-        moved = pltpu.roll(carried, LANES - 16 if source % 2 == 0 else 16, 1)
-        own = own + jnp.where(group == source, jnp.where(head == source, moved, carried), 0.0)
+        here = (group == source) & (head != source)
+        next_to = (group == source ^ 1) & (head == source)
+        for i in range(2):
+            carried = got[(2 + i) * rows : (3 + i) * rows]
+            mixture[i] = mixture[i] + got[i * rows : (i + 1) * rows]
+            own[i] = own[i] + jnp.where(here, carried, 0.0)
+            beside[i] = beside[i] + jnp.where(next_to, carried, 0.0)
+    mixture, own, beside = [left + pltpu.roll(right, 64, 1) for left, right in (mixture, own, beside)]
+    own = own + pltpu.roll(beside, jnp.where(head % 2 == 0, LANES - 16, 16), 1)
     after[...] = own[:, : after.shape[1]].astype(BF16)
     shift = (LANES - width * head) % LANES
     out[...] = pltpu.roll(mixture + own, shift, 1)[:, :width].astype(BF16)

time: 79.5 us -> 79.2 us (level)
  no operation moved by 1% of the time
where the time goes in v5:
time: 79.2 us; the launch traced here: 78.9 us
  blocking collectives  72.6 us (92%)
  Pallas kernels  5.62 us (7%)
    all_to_all x5, blocking collectives, exchange(): return lax.all_to_all(x, axis, 0, 0, tiled=True)  72.6 us
    pallas_call x6, Pallas kernels, call(): pl.pallas_call(body, out_shape=[jax.ShapeDtypeStruct(shape, dtype) if i i...  5.62 us

profile of v5, /device:TPU:1, one launch (start us, length us, event | category | flops | bytes accessed | tf_op | source)
XLA Modules:
  0.0 78.9 jit_solution(7513007733338724531)
XLA Ops:
  0.6 2.1 %shard_map.131 = (bf16[64,2048]{1,0:T(8,128)(2,1)S(1)}, bf16[16,64]{1,0:T(8,128)(2,1)S(1)}, f32[1,4096]{1,0:T(1,128)S(1)}, bf16[320,128]{1,0:T(8,128)(2,1)S(1)},...) custom-call(s32[16]{0:T(128)} %lengths_hbm.1, bf16[16,2048]{1,0:T(8,128)(2,1)} %q_hbm.1, ...), custom_call_target="tpu_custom_call" | custom-call | tf_op jit(solution)/shard_map/pallas_call | solution.py:29
  2.7 10.7 %all_to_all.55 = bf16[8,40,128]{2,1,0:T(8,128)(2,1)S(1)} all-to-all(bf16[8,40,128]{2,1,0:T(8,128)(2,1)S(1)} %bitcast.18), channel_id=1, replica_groups=mesh['far'=8,'near'=8,'head'=4] {'near'}, dimensions={0} | all-to-all | bytes 163840 | tf_op jit(solution)/shard_map/all_to_all | solution.py:261
  13.4 0.2 shard_map.132
  13.6 15.5 %all_to_all.56 = bf16[8,40,128]{2,1,0:T(8,128)(2,1)S(1)} all-to-all(bf16[8,40,128]{2,1,0:T(8,128)(2,1)S(1)} %bitcast.20), channel_id=1, replica_groups=mesh['far'=8,'near'=8,'head'=4] {'far'}, dimensions={0} | all-to-all | bytes 163840 | tf_op jit(solution)/shard_map/all_to_all | solution.py:261
  29.1 0.2 shard_map.133
  29.3 9.3 %all_to_all.57 = bf16[8,32,128]{2,1,0:T(8,128)(2,1)S(1)} all-to-all(bf16[8,32,128]{2,1,0:T(8,128)(2,1)S(1)} %bitcast.23), channel_id=1, replica_groups=mesh['far'=8,'near'=8,'head'=4] {'near'}, dimensions={0} | all-to-all | bytes 131072 | tf_op jit(solution)/shard_map/all_to_all | solution.py:261
  38.7 0.0 copy-start
  38.7 0.0 copy-start.1
  38.7 0.0 copy-start.2
  38.7 0.4 shard_map.134
  39.1 18.9 %all_to_all.58 = bf16[256,2,128]{2,1,0:T(2,128)(2,1)S(1)} all-to-all(bf16[256,2,128]{2,1,0:T(2,128)(2,1)S(1)} %bitcast.17), channel_id=1, replica_groups=mesh['far'=8,'near'=8,'head'=4] {'head','far','near'}, dimensions={0} | all-to-all | bytes 262144 | tf_op jit(solution)/shard_map/all_to_all | solution.py:261
  58.1 0.0 copy-done
  58.1 0.0 copy-done.1
  58.1 0.0 copy-done.2
  58.1 1.7 %shard_map.135 = bf16[512,128]{1,0:T(8,128)(2,1)S(1)} custom-call(bf16[512,128]{1,0:T(8,128)(2,1)S(1)} %bitcast.14, f32[1,4096]{1,0:T(1,128)S(1)} %get-tuple-element.13.gain, bf16[1,4096,384]{2,1,0:T(8,128)(2,1)S(1)} %copy-done, bf16[1,4096,384]{2,1,0:T(8,128)(2,1)S(1)} %copy-done.1, bf16[1,384,4096]{2,1,0:T(8,128)(2,1)S(1)} %copy-done.2, ...), custom_call_target="tpu_custom_call" | custom-call | tf_op jit(solution)/shard_map/pallas_call | solution.py:29
  59.8 18.2 %all_to_all.59 = bf16[256,2,128]{2,1,0:T(2,128)(2,1)S(1)} all-to-all(bf16[256,2,128]{2,1,0:T(2,128)(2,1)S(1)} %bitcast.15), channel_id=1, replica_groups=mesh['far'=8,'near'=8,'head'=4] {'head','far','near'}, dimensions={0} | all-to-all | bytes 262144 | tf_op jit(solution)/shard_map/all_to_all | solution.py:261
  77.9 1.0 %shard_map.136 = (bf16[16,64]{1,0:T(8,128)(2,1)}, bf16[16,16]{1,0:T(8,128)(2,1)}) custom-call(bf16[512,128]{1,0:T(8,128)(2,1)S(1)} %bitcast.16, bf16[64,128]{1,0:T(8,128)(2,1)S(1)} %get-tuple-element.15.turned), custom_call_target="tpu_custom_call" | custom-call | tf_op jit(solution)/shard_map/pallas_call | solution.py:29
Async XLA Ops:
  38.7 19.4 %copy-start = (bf16[1,4096,384]{2,1,0:T(8,128)(2,1)S(1)}, bf16[1,4096,384]{2,1,0:T(8,128)(2,1)}, u32[]{:S(2)}) copy-start(bf16[1,4096,384]{2,1,0:T(8,128)(2,1)} %gate.1) | copy-start | bytes 9437188
  38.7 19.4 %copy-start.1 = (bf16[1,4096,384]{2,1,0:T(8,128)(2,1)S(1)}, bf16[1,4096,384]{2,1,0:T(8,128)(2,1)}, u32[]{:S(2)}) copy-start(bf16[1,4096,384]{2,1,0:T(8,128)(2,1)} %up.1) | copy-start | bytes 9437188
  38.7 19.4 %copy-start.2 = (bf16[1,384,4096]{2,1,0:T(8,128)(2,1)S(1)}, bf16[1,384,4096]{2,1,0:T(8,128)(2,1)}, u32[]{:S(2)}) copy-start(bf16[1,384,4096]{2,1,0:T(8,128)(2,1)} %down.1) | copy-start | bytes 9437188

commit v6 on v5

--- a/solution.py
+++ b/solution.py
@@ -53,10 +53,10 @@
     fetch[0].wait()
     fetch[1].wait()
     routing(ids[...], gates[...], pick, turned, route)
-    fetch[2].wait()
+    for copy in fetch[2:6]:
+        copy.wait()
     for h in range(heads):
         wide[pl.ds(h * rows, rows), :] = q[:, h * HD : (h + 1) * HD].astype(F32)
-    fetch[3].wait()
     scores = [
         lax.dot_general(
             wide[pl.ds(r, heads, stride=rows), :].astype(BF16), k[r], NT, preferred_element_type=F32
@@ -64,13 +64,11 @@
         for r in range(rows)
     ]
     scores = jnp.concatenate(scores, axis=0) * (1.0 / math.sqrt(HD))
-    fetch[4].wait()
     place = own_block() * k.shape[1] + iota((heads, k.shape[1]), 1)
     valid = jnp.concatenate([place < lengths[r] for r in range(rows)], axis=0)
     top = jnp.max(jnp.where(valid, scores, MASKED), axis=1, keepdims=True).astype(BF16).astype(F32)
     weights = jnp.where(valid, jnp.exp(scores - top), 0.0).astype(BF16)
     total = jnp.sum(weights.astype(F32), axis=1, keepdims=True)
-    fetch[5].wait()
     numer = [
         jnp.dot(weights[r * heads : (r + 1) * heads], v[r], preferred_element_type=F32)
         for r in range(rows)
@@ -204,7 +202,8 @@
     summed = pieces[:half].astype(F32)
     for i in range(1, heads):
         summed = summed + pieces[i * half : (i + 1) * half].astype(F32)
-    stacked = swap(summed).astype(BF16).astype(F32)
+    summed = summed.astype(BF16).astype(F32)
+    stacked = swap(summed)
     tiles = []
     for b in range(blocks):
         tile = stacked[8 * (b // 2) : 8 * (b // 2) + 8]
@@ -223,14 +222,13 @@
         left = result[:, b * LANES : (b + 1) * LANES]
         right = result[:, (b + 1) * LANES : (b + 2) * LANES]
         pairs.append(jnp.where(lower, left, pltpu.roll(right, 4, 0)))
-    mixed = jnp.concatenate(pairs, axis=0)
+    mixed = swap(jnp.concatenate(pairs, axis=0))
     head = lax.axis_index("head")
     group = iota(mixed.shape, 1) // 16 % heads
-    moved = pltpu.roll(stacked, jnp.where(head % 2 == 0, 16, LANES - 16), 1)
+    moved = pltpu.roll(summed, jnp.where(head % 2 == 0, 16, LANES - 16), 1)
     for target in range(heads):
-        carried = jnp.where(target == head, moved, stacked)
-        packed = swap(jnp.where(group == target, mixed, carried))
-        out[pl.ds(target * half, half), :] = packed.astype(BF16)
+        carried = jnp.where(target == head, moved, summed)
+        out[pl.ds(target * half, half), :] = jnp.where(group == target, mixed, carried).astype(BF16)
 
 
 def finish(pieces, turned, after, out):

time: 79.2 us -> 79.1 us (level)
  no operation moved by 1% of the time
where the time goes in v6:
time: 79.1 us; the launch traced here: 78.8 us
  blocking collectives  72.6 us (92%)
  Pallas kernels  5.5 us (7%)
    all_to_all x5, blocking collectives, exchange(): return lax.all_to_all(x, axis, 0, 0, tiled=True)  72.6 us
    pallas_call x6, Pallas kernels, call(): pl.pallas_call(body, out_shape=[jax.ShapeDtypeStruct(shape, dtype) if i i...  5.5 us

profile of v6, /device:TPU:1, one launch (start us, length us, event | category | flops | bytes accessed | tf_op | source)
XLA Modules:
  0.0 78.8 jit_solution(4097406400153499089)
XLA Ops:
  0.6 2.0 %shard_map.131 = (bf16[64,2048]{1,0:T(8,128)(2,1)S(1)}, bf16[16,64]{1,0:T(8,128)(2,1)S(1)}, f32[1,4096]{1,0:T(1,128)S(1)}, bf16[320,128]{1,0:T(8,128)(2,1)S(1)},...) custom-call(s32[16]{0:T(128)} %lengths_hbm.1, bf16[16,2048]{1,0:T(8,128)(2,1)} %q_hbm.1, ...), custom_call_target="tpu_custom_call" | custom-call | tf_op jit(solution)/shard_map/pallas_call | solution.py:29
  2.6 10.7 %all_to_all.55 = bf16[8,40,128]{2,1,0:T(8,128)(2,1)S(1)} all-to-all(bf16[8,40,128]{2,1,0:T(8,128)(2,1)S(1)} %bitcast.18), channel_id=1, replica_groups=mesh['far'=8,'near'=8,'head'=4] {'near'}, dimensions={0} | all-to-all | bytes 163840 | tf_op jit(solution)/shard_map/all_to_all | solution.py:259
  13.3 0.2 shard_map.132
  13.5 15.5 %all_to_all.56 = bf16[8,40,128]{2,1,0:T(8,128)(2,1)S(1)} all-to-all(bf16[8,40,128]{2,1,0:T(8,128)(2,1)S(1)} %bitcast.20), channel_id=1, replica_groups=mesh['far'=8,'near'=8,'head'=4] {'far'}, dimensions={0} | all-to-all | bytes 163840 | tf_op jit(solution)/shard_map/all_to_all | solution.py:259
  29.0 0.2 shard_map.133
  29.2 9.3 %all_to_all.57 = bf16[8,32,128]{2,1,0:T(8,128)(2,1)S(1)} all-to-all(bf16[8,32,128]{2,1,0:T(8,128)(2,1)S(1)} %bitcast.23), channel_id=1, replica_groups=mesh['far'=8,'near'=8,'head'=4] {'near'}, dimensions={0} | all-to-all | bytes 131072 | tf_op jit(solution)/shard_map/all_to_all | solution.py:259
  38.6 0.0 copy-start
  38.6 0.0 copy-start.1
  38.6 0.0 copy-start.2
  38.6 0.4 shard_map.134
  39.0 18.9 %all_to_all.58 = bf16[256,2,128]{2,1,0:T(2,128)(2,1)S(1)} all-to-all(bf16[256,2,128]{2,1,0:T(2,128)(2,1)S(1)} %bitcast.17), channel_id=1, replica_groups=mesh['far'=8,'near'=8,'head'=4] {'head','far','near'}, dimensions={0} | all-to-all | bytes 262144 | tf_op jit(solution)/shard_map/all_to_all | solution.py:259
  58.0 0.0 copy-done
  58.0 0.0 copy-done.1
  58.0 0.0 copy-done.2
  58.0 1.7 %shard_map.135 = bf16[512,128]{1,0:T(8,128)(2,1)S(1)} custom-call(bf16[512,128]{1,0:T(8,128)(2,1)S(1)} %bitcast.14, f32[1,4096]{1,0:T(1,128)S(1)} %get-tuple-element.13.gain, bf16[1,4096,384]{2,1,0:T(8,128)(2,1)S(1)} %copy-done, bf16[1,4096,384]{2,1,0:T(8,128)(2,1)S(1)} %copy-done.1, bf16[1,384,4096]{2,1,0:T(8,128)(2,1)S(1)} %copy-done.2, ...), custom_call_target="tpu_custom_call" | custom-call | tf_op jit(solution)/shard_map/pallas_call | solution.py:29
  59.7 18.2 %all_to_all.59 = bf16[256,2,128]{2,1,0:T(2,128)(2,1)S(1)} all-to-all(bf16[256,2,128]{2,1,0:T(2,128)(2,1)S(1)} %bitcast.15), channel_id=1, replica_groups=mesh['far'=8,'near'=8,'head'=4] {'head','far','near'}, dimensions={0} | all-to-all | bytes 262144 | tf_op jit(solution)/shard_map/all_to_all | solution.py:259
  77.8 1.0 %shard_map.136 = (bf16[16,64]{1,0:T(8,128)(2,1)}, bf16[16,16]{1,0:T(8,128)(2,1)}) custom-call(bf16[512,128]{1,0:T(8,128)(2,1)S(1)} %bitcast.16, bf16[64,128]{1,0:T(8,128)(2,1)S(1)} %get-tuple-element.15.turned), custom_call_target="tpu_custom_call" | custom-call | tf_op jit(solution)/shard_map/pallas_call | solution.py:29
Async XLA Ops:
  38.6 19.4 %copy-start = (bf16[1,4096,384]{2,1,0:T(8,128)(2,1)S(1)}, bf16[1,4096,384]{2,1,0:T(8,128)(2,1)}, u32[]{:S(2)}) copy-start(bf16[1,4096,384]{2,1,0:T(8,128)(2,1)} %gate.1) | copy-start | bytes 9437188
  38.6 19.4 %copy-start.1 = (bf16[1,4096,384]{2,1,0:T(8,128)(2,1)S(1)}, bf16[1,4096,384]{2,1,0:T(8,128)(2,1)}, u32[]{:S(2)}) copy-start(bf16[1,4096,384]{2,1,0:T(8,128)(2,1)} %up.1) | copy-start | bytes 9437188
  38.6 19.4 %copy-start.2 = (bf16[1,384,4096]{2,1,0:T(8,128)(2,1)S(1)}, bf16[1,384,4096]{2,1,0:T(8,128)(2,1)}, u32[]{:S(2)}) copy-start(bf16[1,384,4096]{2,1,0:T(8,128)(2,1)} %down.1) | copy-start | bytes 9437188

commit v7 on v6

--- a/solution.py
+++ b/solution.py
@@ -210,9 +210,10 @@
         tiles.append(tile if b % 2 == 0 else pltpu.roll(tile, 4, 0))
     x = jnp.concatenate(tiles, axis=1)
     square = jnp.sum(x * x, axis=1, keepdims=True) * (1.0 / width)
-    normed = (x * lax.rsqrt(square + 1e-6) * gain[...]).astype(BF16)
-    gate_proj = jnp.dot(normed, gate[0], preferred_element_type=F32)
-    up_proj = jnp.dot(normed, up[0], preferred_element_type=F32)
+    scale = lax.rsqrt(square + 1e-6)
+    scaled = (x * gain[...]).astype(BF16)
+    gate_proj = jnp.dot(scaled, gate[0], preferred_element_type=F32) * scale
+    up_proj = jnp.dot(scaled, up[0], preferred_element_type=F32) * scale
     hidden = (gate_proj / (1.0 + jnp.exp(-gate_proj)) * up_proj).astype(BF16)
     result = jnp.dot(hidden, down[0], preferred_element_type=F32) * route[:, 0:1]
 

time: 79.1 us -> 79 us (level)
  no operation moved by 1% of the time
where the time goes in v7:
time: 79 us; the launch traced here: 78.7 us
  blocking collectives  72.6 us (92%)
  Pallas kernels  5.38 us (7%)
    all_to_all x5, blocking collectives, exchange(): return lax.all_to_all(x, axis, 0, 0, tiled=True)  72.6 us
    pallas_call x6, Pallas kernels, call(): pl.pallas_call(body, out_shape=[jax.ShapeDtypeStruct(shape, dtype) if i i...  5.38 us

profile of v7, /device:TPU:1, one launch (start us, length us, event | category | flops | bytes accessed | tf_op | source)
XLA Modules:
  0.0 78.7 jit_solution(231141518707888895)
XLA Ops:
  0.6 2.0 %shard_map.131 = (bf16[64,2048]{1,0:T(8,128)(2,1)S(1)}, bf16[16,64]{1,0:T(8,128)(2,1)S(1)}, f32[1,4096]{1,0:T(1,128)S(1)}, bf16[320,128]{1,0:T(8,128)(2,1)S(1)},...) custom-call(s32[16]{0:T(128)} %lengths_hbm.1, bf16[16,2048]{1,0:T(8,128)(2,1)} %q_hbm.1, ...), custom_call_target="tpu_custom_call" | custom-call | tf_op jit(solution)/shard_map/pallas_call | solution.py:29
  2.6 10.7 %all_to_all.55 = bf16[8,40,128]{2,1,0:T(8,128)(2,1)S(1)} all-to-all(bf16[8,40,128]{2,1,0:T(8,128)(2,1)S(1)} %bitcast.18), channel_id=1, replica_groups=mesh['far'=8,'near'=8,'head'=4] {'near'}, dimensions={0} | all-to-all | bytes 163840 | tf_op jit(solution)/shard_map/all_to_all | solution.py:260
  13.3 0.2 shard_map.132
  13.5 15.5 %all_to_all.56 = bf16[8,40,128]{2,1,0:T(8,128)(2,1)S(1)} all-to-all(bf16[8,40,128]{2,1,0:T(8,128)(2,1)S(1)} %bitcast.20), channel_id=1, replica_groups=mesh['far'=8,'near'=8,'head'=4] {'far'}, dimensions={0} | all-to-all | bytes 163840 | tf_op jit(solution)/shard_map/all_to_all | solution.py:260
  29.0 0.2 shard_map.133
  29.2 9.3 %all_to_all.57 = bf16[8,32,128]{2,1,0:T(8,128)(2,1)S(1)} all-to-all(bf16[8,32,128]{2,1,0:T(8,128)(2,1)S(1)} %bitcast.23), channel_id=1, replica_groups=mesh['far'=8,'near'=8,'head'=4] {'near'}, dimensions={0} | all-to-all | bytes 131072 | tf_op jit(solution)/shard_map/all_to_all | solution.py:260
  38.6 0.0 copy-start
  38.6 0.0 copy-start.1
  38.6 0.0 copy-start.2
  38.6 0.4 shard_map.134
  39.0 18.9 %all_to_all.58 = bf16[256,2,128]{2,1,0:T(2,128)(2,1)S(1)} all-to-all(bf16[256,2,128]{2,1,0:T(2,128)(2,1)S(1)} %bitcast.17), channel_id=1, replica_groups=mesh['far'=8,'near'=8,'head'=4] {'head','far','near'}, dimensions={0} | all-to-all | bytes 262144 | tf_op jit(solution)/shard_map/all_to_all | solution.py:260
  58.0 0.0 copy-done
  58.0 0.0 copy-done.1
  58.0 0.0 copy-done.2
  58.0 1.6 %shard_map.135 = bf16[512,128]{1,0:T(8,128)(2,1)S(1)} custom-call(bf16[512,128]{1,0:T(8,128)(2,1)S(1)} %bitcast.14, f32[1,4096]{1,0:T(1,128)S(1)} %get-tuple-element.13.gain, bf16[1,4096,384]{2,1,0:T(8,128)(2,1)S(1)} %copy-done, bf16[1,4096,384]{2,1,0:T(8,128)(2,1)S(1)} %copy-done.1, bf16[1,384,4096]{2,1,0:T(8,128)(2,1)S(1)} %copy-done.2, ...), custom_call_target="tpu_custom_call" | custom-call | tf_op jit(solution)/shard_map/pallas_call | solution.py:29
  59.5 18.2 %all_to_all.59 = bf16[256,2,128]{2,1,0:T(2,128)(2,1)S(1)} all-to-all(bf16[256,2,128]{2,1,0:T(2,128)(2,1)S(1)} %bitcast.15), channel_id=1, replica_groups=mesh['far'=8,'near'=8,'head'=4] {'head','far','near'}, dimensions={0} | all-to-all | bytes 262144 | tf_op jit(solution)/shard_map/all_to_all | solution.py:260
  77.7 1.0 %shard_map.136 = (bf16[16,64]{1,0:T(8,128)(2,1)}, bf16[16,16]{1,0:T(8,128)(2,1)}) custom-call(bf16[512,128]{1,0:T(8,128)(2,1)S(1)} %bitcast.16, bf16[64,128]{1,0:T(8,128)(2,1)S(1)} %get-tuple-element.15.turned), custom_call_target="tpu_custom_call" | custom-call | tf_op jit(solution)/shard_map/pallas_call | solution.py:29
Async XLA Ops:
  38.6 19.4 %copy-start = (bf16[1,4096,384]{2,1,0:T(8,128)(2,1)S(1)}, bf16[1,4096,384]{2,1,0:T(8,128)(2,1)}, u32[]{:S(2)}) copy-start(bf16[1,4096,384]{2,1,0:T(8,128)(2,1)} %gate.1) | copy-start | bytes 9437188
  38.6 19.4 %copy-start.1 = (bf16[1,4096,384]{2,1,0:T(8,128)(2,1)S(1)}, bf16[1,4096,384]{2,1,0:T(8,128)(2,1)}, u32[]{:S(2)}) copy-start(bf16[1,4096,384]{2,1,0:T(8,128)(2,1)} %up.1) | copy-start | bytes 9437188
  38.6 19.4 %copy-start.2 = (bf16[1,384,4096]{2,1,0:T(8,128)(2,1)S(1)}, bf16[1,384,4096]{2,1,0:T(8,128)(2,1)}, u32[]{:S(2)}) copy-start(bf16[1,384,4096]{2,1,0:T(8,128)(2,1)} %down.1) | copy-start | bytes 9437188

commit v8 on v7

--- a/solution.py
+++ b/solution.py
@@ -158,7 +158,12 @@
     lhs = jnp.concatenate(
         [wide[pl.ds(h, rows, stride=heads), :].astype(BF16) for h in range(heads)], axis=1
     )
-    part = lax.dot_general(lhs, weight[...], NT, preferred_element_type=F32)
+    depth = lhs.shape[1] // 4
+    quarters = [
+        lax.dot_general(lhs[:, i : i + depth], weight[:, i : i + depth], NT, preferred_element_type=F32)
+        for i in range(0, lhs.shape[1], depth)
+    ]
+    part = (quarters[0] + quarters[1]) + (quarters[2] + quarters[3])
     part = part + jnp.where(lax.axis_index("head") == 0, residual[...].astype(F32), 0.0)
     none = jnp.zeros_like(part)
     twice = jnp.concatenate(

time: 79 us -> 78.9 us (level)
  no operation moved by 1% of the time
where the time goes in v8:
time: 78.9 us; the launch traced here: 78.6 us
  blocking collectives  72.6 us (92%)
  Pallas kernels  5.36 us (7%)
    all_to_all x5, blocking collectives, exchange(): return lax.all_to_all(x, axis, 0, 0, tiled=True)  72.6 us
    pallas_call x6, Pallas kernels, call(): pl.pallas_call(body, out_shape=[jax.ShapeDtypeStruct(shape, dtype) if i i...  5.36 us

profile of v8, /device:TPU:1, one launch (start us, length us, event | category | flops | bytes accessed | tf_op | source)
XLA Modules:
  0.0 78.6 jit_solution(12923349009420791300)
XLA Ops:
  0.6 2.0 %shard_map.131 = (bf16[64,2048]{1,0:T(8,128)(2,1)S(1)}, bf16[16,64]{1,0:T(8,128)(2,1)S(1)}, f32[1,4096]{1,0:T(1,128)S(1)}, bf16[320,128]{1,0:T(8,128)(2,1)S(1)},...) custom-call(s32[16]{0:T(128)} %lengths_hbm.1, bf16[16,2048]{1,0:T(8,128)(2,1)} %q_hbm.1, ...), custom_call_target="tpu_custom_call" | custom-call | tf_op jit(solution)/shard_map/pallas_call | solution.py:29
  2.6 10.7 %all_to_all.55 = bf16[8,40,128]{2,1,0:T(8,128)(2,1)S(1)} all-to-all(bf16[8,40,128]{2,1,0:T(8,128)(2,1)S(1)} %bitcast.18), channel_id=1, replica_groups=mesh['far'=8,'near'=8,'head'=4] {'near'}, dimensions={0} | all-to-all | bytes 163840 | tf_op jit(solution)/shard_map/all_to_all | solution.py:265
  13.3 0.2 shard_map.132
  13.5 15.5 %all_to_all.56 = bf16[8,40,128]{2,1,0:T(8,128)(2,1)S(1)} all-to-all(bf16[8,40,128]{2,1,0:T(8,128)(2,1)S(1)} %bitcast.20), channel_id=1, replica_groups=mesh['far'=8,'near'=8,'head'=4] {'far'}, dimensions={0} | all-to-all | bytes 163840 | tf_op jit(solution)/shard_map/all_to_all | solution.py:265
  29.0 0.2 shard_map.133
  29.2 9.3 %all_to_all.57 = bf16[8,32,128]{2,1,0:T(8,128)(2,1)S(1)} all-to-all(bf16[8,32,128]{2,1,0:T(8,128)(2,1)S(1)} %bitcast.23), channel_id=1, replica_groups=mesh['far'=8,'near'=8,'head'=4] {'near'}, dimensions={0} | all-to-all | bytes 131072 | tf_op jit(solution)/shard_map/all_to_all | solution.py:265
  38.6 0.0 copy-start
  38.6 0.0 copy-start.1
  38.6 0.0 copy-start.2
  38.6 0.4 shard_map.134
  39.0 18.9 %all_to_all.58 = bf16[256,2,128]{2,1,0:T(2,128)(2,1)S(1)} all-to-all(bf16[256,2,128]{2,1,0:T(2,128)(2,1)S(1)} %bitcast.17), channel_id=1, replica_groups=mesh['far'=8,'near'=8,'head'=4] {'head','far','near'}, dimensions={0} | all-to-all | bytes 262144 | tf_op jit(solution)/shard_map/all_to_all | solution.py:265
  57.9 0.0 copy-done
  57.9 0.0 copy-done.1
  57.9 0.0 copy-done.2
  57.9 1.6 %shard_map.135 = bf16[512,128]{1,0:T(8,128)(2,1)S(1)} custom-call(bf16[512,128]{1,0:T(8,128)(2,1)S(1)} %bitcast.14, f32[1,4096]{1,0:T(1,128)S(1)} %get-tuple-element.13.gain, bf16[1,4096,384]{2,1,0:T(8,128)(2,1)S(1)} %copy-done, bf16[1,4096,384]{2,1,0:T(8,128)(2,1)S(1)} %copy-done.1, bf16[1,384,4096]{2,1,0:T(8,128)(2,1)S(1)} %copy-done.2, ...), custom_call_target="tpu_custom_call" | custom-call | tf_op jit(solution)/shard_map/pallas_call | solution.py:29
  59.5 18.2 %all_to_all.59 = bf16[256,2,128]{2,1,0:T(2,128)(2,1)S(1)} all-to-all(bf16[256,2,128]{2,1,0:T(2,128)(2,1)S(1)} %bitcast.15), channel_id=1, replica_groups=mesh['far'=8,'near'=8,'head'=4] {'head','far','near'}, dimensions={0} | all-to-all | bytes 262144 | tf_op jit(solution)/shard_map/all_to_all | solution.py:265
  77.7 1.0 %shard_map.136 = (bf16[16,64]{1,0:T(8,128)(2,1)}, bf16[16,16]{1,0:T(8,128)(2,1)}) custom-call(bf16[512,128]{1,0:T(8,128)(2,1)S(1)} %bitcast.16, bf16[64,128]{1,0:T(8,128)(2,1)S(1)} %get-tuple-element.15.turned), custom_call_target="tpu_custom_call" | custom-call | tf_op jit(solution)/shard_map/pallas_call | solution.py:29
Async XLA Ops:
  38.6 19.3 %copy-start = (bf16[1,4096,384]{2,1,0:T(8,128)(2,1)S(1)}, bf16[1,4096,384]{2,1,0:T(8,128)(2,1)}, u32[]{:S(2)}) copy-start(bf16[1,4096,384]{2,1,0:T(8,128)(2,1)} %gate.1) | copy-start | bytes 9437188
  38.6 19.3 %copy-start.1 = (bf16[1,4096,384]{2,1,0:T(8,128)(2,1)S(1)}, bf16[1,4096,384]{2,1,0:T(8,128)(2,1)}, u32[]{:S(2)}) copy-start(bf16[1,4096,384]{2,1,0:T(8,128)(2,1)} %up.1) | copy-start | bytes 9437188
  38.6 19.3 %copy-start.2 = (bf16[1,384,4096]{2,1,0:T(8,128)(2,1)S(1)}, bf16[1,384,4096]{2,1,0:T(8,128)(2,1)}, u32[]{:S(2)}) copy-start(bf16[1,384,4096]{2,1,0:T(8,128)(2,1)} %down.1) | copy-start | bytes 9437188

commit v9 on v8

--- a/solution.py
+++ b/solution.py
@@ -158,12 +158,14 @@
     lhs = jnp.concatenate(
         [wide[pl.ds(h, rows, stride=heads), :].astype(BF16) for h in range(heads)], axis=1
     )
-    depth = lhs.shape[1] // 4
-    quarters = [
+    depth = lhs.shape[1] // 8
+    sums = [
         lax.dot_general(lhs[:, i : i + depth], weight[:, i : i + depth], NT, preferred_element_type=F32)
         for i in range(0, lhs.shape[1], depth)
     ]
-    part = (quarters[0] + quarters[1]) + (quarters[2] + quarters[3])
+    while len(sums) > 1:
+        sums = [left + right for left, right in zip(sums[::2], sums[1::2])]
+    part = sums[0]
     part = part + jnp.where(lax.axis_index("head") == 0, residual[...].astype(F32), 0.0)
     none = jnp.zeros_like(part)
     twice = jnp.concatenate(

time: 78.9 us -> 78.9 us (level)
  no operation moved by 1% of the time
where the time goes in v9:
time: 78.9 us; the launch traced here: 78.6 us
  blocking collectives  72.6 us (92%)
  Pallas kernels  5.36 us (7%)
    all_to_all x5, blocking collectives, exchange(): return lax.all_to_all(x, axis, 0, 0, tiled=True)  72.6 us
    pallas_call x6, Pallas kernels, call(): pl.pallas_call(body, out_shape=[jax.ShapeDtypeStruct(shape, dtype) if i i...  5.36 us

profile of v9, /device:TPU:1, one launch (start us, length us, event | category | flops | bytes accessed | tf_op | source)
XLA Modules:
  0.0 78.6 jit_solution(16367894396396285986)
XLA Ops:
  0.6 2.0 %shard_map.131 = (bf16[64,2048]{1,0:T(8,128)(2,1)S(1)}, bf16[16,64]{1,0:T(8,128)(2,1)S(1)}, f32[1,4096]{1,0:T(1,128)S(1)}, bf16[320,128]{1,0:T(8,128)(2,1)S(1)},...) custom-call(s32[16]{0:T(128)} %lengths_hbm.1, bf16[16,2048]{1,0:T(8,128)(2,1)} %q_hbm.1, ...), custom_call_target="tpu_custom_call" | custom-call | tf_op jit(solution)/shard_map/pallas_call | solution.py:29
  2.6 10.7 %all_to_all.55 = bf16[8,40,128]{2,1,0:T(8,128)(2,1)S(1)} all-to-all(bf16[8,40,128]{2,1,0:T(8,128)(2,1)S(1)} %bitcast.18), channel_id=1, replica_groups=mesh['far'=8,'near'=8,'head'=4] {'near'}, dimensions={0} | all-to-all | bytes 163840 | tf_op jit(solution)/shard_map/all_to_all | solution.py:267
  13.3 0.2 shard_map.132
  13.5 15.5 %all_to_all.56 = bf16[8,40,128]{2,1,0:T(8,128)(2,1)S(1)} all-to-all(bf16[8,40,128]{2,1,0:T(8,128)(2,1)S(1)} %bitcast.20), channel_id=1, replica_groups=mesh['far'=8,'near'=8,'head'=4] {'far'}, dimensions={0} | all-to-all | bytes 163840 | tf_op jit(solution)/shard_map/all_to_all | solution.py:267
  29.0 0.2 shard_map.133
  29.2 9.3 %all_to_all.57 = bf16[8,32,128]{2,1,0:T(8,128)(2,1)S(1)} all-to-all(bf16[8,32,128]{2,1,0:T(8,128)(2,1)S(1)} %bitcast.23), channel_id=1, replica_groups=mesh['far'=8,'near'=8,'head'=4] {'near'}, dimensions={0} | all-to-all | bytes 131072 | tf_op jit(solution)/shard_map/all_to_all | solution.py:267
  38.6 0.0 copy-start
  38.6 0.0 copy-start.1
  38.6 0.0 copy-start.2
  38.6 0.4 shard_map.134
  39.0 18.9 %all_to_all.58 = bf16[256,2,128]{2,1,0:T(2,128)(2,1)S(1)} all-to-all(bf16[256,2,128]{2,1,0:T(2,128)(2,1)S(1)} %bitcast.17), channel_id=1, replica_groups=mesh['far'=8,'near'=8,'head'=4] {'head','far','near'}, dimensions={0} | all-to-all | bytes 262144 | tf_op jit(solution)/shard_map/all_to_all | solution.py:267
  57.9 0.0 copy-done
  57.9 0.0 copy-done.1
  57.9 0.0 copy-done.2
  57.9 1.6 %shard_map.135 = bf16[512,128]{1,0:T(8,128)(2,1)S(1)} custom-call(bf16[512,128]{1,0:T(8,128)(2,1)S(1)} %bitcast.14, f32[1,4096]{1,0:T(1,128)S(1)} %get-tuple-element.13.gain, bf16[1,4096,384]{2,1,0:T(8,128)(2,1)S(1)} %copy-done, bf16[1,4096,384]{2,1,0:T(8,128)(2,1)S(1)} %copy-done.1, bf16[1,384,4096]{2,1,0:T(8,128)(2,1)S(1)} %copy-done.2, ...), custom_call_target="tpu_custom_call" | custom-call | tf_op jit(solution)/shard_map/pallas_call | solution.py:29
  59.5 18.2 %all_to_all.59 = bf16[256,2,128]{2,1,0:T(2,128)(2,1)S(1)} all-to-all(bf16[256,2,128]{2,1,0:T(2,128)(2,1)S(1)} %bitcast.15), channel_id=1, replica_groups=mesh['far'=8,'near'=8,'head'=4] {'head','far','near'}, dimensions={0} | all-to-all | bytes 262144 | tf_op jit(solution)/shard_map/all_to_all | solution.py:267
  77.7 1.0 %shard_map.136 = (bf16[16,64]{1,0:T(8,128)(2,1)}, bf16[16,16]{1,0:T(8,128)(2,1)}) custom-call(bf16[512,128]{1,0:T(8,128)(2,1)S(1)} %bitcast.16, bf16[64,128]{1,0:T(8,128)(2,1)S(1)} %get-tuple-element.15.turned), custom_call_target="tpu_custom_call" | custom-call | tf_op jit(solution)/shard_map/pallas_call | solution.py:29
Async XLA Ops:
  38.6 19.3 %copy-start = (bf16[1,4096,384]{2,1,0:T(8,128)(2,1)S(1)}, bf16[1,4096,384]{2,1,0:T(8,128)(2,1)}, u32[]{:S(2)}) copy-start(bf16[1,4096,384]{2,1,0:T(8,128)(2,1)} %gate.1) | copy-start | bytes 9437188
  38.6 19.3 %copy-start.1 = (bf16[1,4096,384]{2,1,0:T(8,128)(2,1)S(1)}, bf16[1,4096,384]{2,1,0:T(8,128)(2,1)}, u32[]{:S(2)}) copy-start(bf16[1,4096,384]{2,1,0:T(8,128)(2,1)} %up.1) | copy-start | bytes 9437188
  38.6 19.3 %copy-start.2 = (bf16[1,384,4096]{2,1,0:T(8,128)(2,1)S(1)}, bf16[1,384,4096]{2,1,0:T(8,128)(2,1)}, u32[]{:S(2)}) copy-start(bf16[1,384,4096]{2,1,0:T(8,128)(2,1)} %down.1) | copy-start | bytes 9437188
